TPU v7x, 128 devices: a whole 4x4x4 slice. The times are simulated.
128 devices in a mesh: dp: 16 (over x_hi, z, core), tensor: 8 (over x_lo, y).
Axes of the slice: x: 4 (x_hi: 2, x_lo: 2; x = x_hi * 2 + x_lo), y: 4, z: 4, core: 2. Of those that a mesh axis runs over, the one named last changes fastest.
Arguments:
- query_states: bfloat16 [4608, 3584], P('dp', 'tensor'), may hold values from -256 to 256, as said below
- doc_states: bfloat16 [4608, 3584], P('dp', 'tensor'), may hold values from -256 to 256, as said below
- gain: float32 [3584], P('tensor'), may hold values from 0.5 to 1.5
- positives: int32 [4608], P('dp'), may hold values from 0 to 4607, each once
Outputs:
- grad_query: bfloat16 [4608, 3584], P('dp', 'tensor')
- grad_doc: bfloat16 [4608, 3584], P('dp', 'tensor')
- grad_gain: float32 [3584], P('tensor')
- loss: float32 [], replicated
Inputs may be any that keep to these rules, and one draw needn't show every extreme that they name: `query_states`: finite hidden states. `doc_states`: finite hidden states.
All inputs are finite; a program needn't handle non-finite values.
Results may differ from a plain program's by a relative error of at most 0.0066.
Values may be sent and summed in bfloat16 or wider, within the bound.
A program may use at most 128 MiB of HBM per device.

v0:
```python
import jax
import jax.numpy as jnp
from jax import lax
from jax.sharding import PartitionSpec as P

eps_len = 1e-06
inv_temp = 100.0
masked = -1e30


def contract_cols(left, right):
    return lax.dot_general(
        left, right, (((1,), (1,)), ((), ())), preferred_element_type=jnp.float32
    )


def contract_rows(left, right):
    return lax.dot_general(
        left, right, (((0,), (0,)), ((), ())), preferred_element_type=jnp.float32
    )


def shards(query_states, doc_states, gain, positives):
    rows, feats = query_states.shape
    hq = query_states.astype(jnp.float32)
    hd = doc_states.astype(jnp.float32)
    normed_q = hq * gain[None, :]
    normed_d = hd * gain[None, :]
    length_q, length_d = lax.psum(
        (jnp.sum(normed_q * normed_q, axis=1), jnp.sum(normed_d * normed_d, axis=1)), "tensor"
    )
    inverse_q = lax.rsqrt(length_q + eps_len)
    inverse_d = lax.rsqrt(length_d + eps_len)
    query_emb = (normed_q * inverse_q[:, None]).astype(jnp.bfloat16)
    doc_emb = (normed_d * inverse_d[:, None]).astype(jnp.bfloat16)
    all_query, all_doc = (
        lax.all_gather(query_emb, "dp", axis=0, tiled=True),
        lax.all_gather(doc_emb, "dp", axis=0, tiled=True),
    )
    pairs = all_doc.shape[0]
    part_d = contract_cols(query_emb, all_doc) * inv_temp
    part_q = contract_cols(query_emb, all_query) * inv_temp
    own_rows = lax.axis_index("dp") * rows + lax.iota(jnp.int32, rows)
    logit_d, logit_q = lax.psum((part_d, part_q), "tensor")
    column = lax.iota(jnp.int32, pairs)
    logit_q = jnp.where(own_rows[:, None] == column[None, :], masked, logit_q)
    hit = positives[:, None] == column[None, :]
    top = jnp.maximum(jnp.max(logit_d, axis=1), jnp.max(logit_q, axis=1))
    total = jnp.sum(jnp.exp(logit_d - top[:, None]), axis=1) + jnp.sum(
        jnp.exp(logit_q - top[:, None]), axis=1
    )
    posit = jnp.sum(jnp.where(hit, logit_d, 0.0), axis=1)
    lse = top + jnp.log(total)
    weight_d = ((jnp.exp(logit_d - lse[:, None]) - hit.astype(jnp.float32)) / pairs).astype(
        jnp.bfloat16
    )
    weight_q = (jnp.exp(logit_q - lse[:, None]) / pairs).astype(jnp.bfloat16)
    loss_rows = jnp.sum(lse - posit)
    local_q = (
        jnp.dot(weight_d, all_doc, preferred_element_type=jnp.float32)
        + jnp.dot(weight_q, all_query, preferred_element_type=jnp.float32)
    ) * inv_temp
    returned = lax.psum_scatter(
        jnp.concatenate(
            [contract_rows(weight_d, query_emb), contract_rows(weight_q, query_emb)], axis=1
        )
        * inv_temp,
        "dp",
        scatter_dimension=0,
        tiled=True,
    )
    grad_emb_d = returned[:, :feats]
    grad_emb_q = local_q + returned[:, feats:]
    first_q, first_d = lax.psum(
        (jnp.sum(grad_emb_q * normed_q, axis=1), jnp.sum(grad_emb_d * normed_d, axis=1)), "tensor"
    )
    grad_x_q = inverse_q[:, None] * grad_emb_q - normed_q * (inverse_q**3 * first_q)[:, None]
    grad_x_d = inverse_d[:, None] * grad_emb_d - normed_d * (inverse_d**3 * first_d)[:, None]
    grad_hq = grad_x_q * gain[None, :]
    grad_hd = grad_x_d * gain[None, :]
    gain_local = jnp.sum(grad_x_q * hq, axis=0) + jnp.sum(grad_x_d * hd, axis=0)
    grad_gain, loss_sum = lax.psum((gain_local, loss_rows), "dp")
    return (grad_hq.astype(jnp.bfloat16), grad_hd.astype(jnp.bfloat16), grad_gain, loss_sum / pairs)


def solution(mesh):
    return jax.shard_map(
        shards,
        mesh=mesh,
        in_specs=(P("dp", "tensor"), P("dp", "tensor"), P("tensor"), P("dp")),
        out_specs=(P("dp", "tensor"), P("dp", "tensor"), P("tensor"), P()),
        check_vma=False,
    )
```

profile of v0, /device:TPU:1, one launch (start us, length us, event | category | flops | bytes accessed | tf_op | source)
XLA Modules:
  0.0 618.9 jit_solution(3866370949951124343)
XLA Ops:
  7.2 1.3 fusion.17
  8.5 17.0 %all-reduce.2 = (f32[288]{0:T(512)S(1)}, f32[288]{0:T(512)S(1)}) all-reduce(f32[288]{0:T(512)S(1)} %get-tuple-element.12, f32[288]{0:T(512)S(1)} %get-tuple-element.11), channel_id=1, replica_groups=mesh['dp'=16,'tensor'=8] {'tensor'}, use_global_device_ids=true, to_apply=%region_1.0 | all-reduce | flops 576 | bytes 4608 | tf_op jit(solution)/shard_map/psum | solution.py:29
  25.5 2.0 fusion.18
  27.6 0.7 all-gather.3.cloned.1.call-update
  28.4 60.7 %all-gather.5.cloned.1.call-done = bf16[4608,448]{1,0:T(8,128)(2,1)} async-done(((bf16[288,448]{1,0:T(8,128)(2,1)}), bf16[4608,448]{1,0:T(8,128)(2,1)}) %all-gather.5.cloned.1.call-update) | async-done | bytes 4128784 | tf_op jit(solution)/shard_map/all_gather | solution.py:37
  89.1 6.4 %convolution_multiply_fusion = f32[288,4608]{1,0:T(8,128)} fusion(bf16[288,448]{1,0:T(8,128)(2,1)} %get-tuple-element.26, bf16[4608,448]{1,0:T(8,128)(2,1)} %all-gather.5.cloned.1.call-done), kind=kOutput, calls=%fused_computation.1 | convolution fusion | flops 1190412288 | bytes 9695232 | tf_op jit(solution)/shard_map/dot_general | solution.py:12
  95.5 52.1 %all-gather.3.cloned.1.call-done = bf16[4608,448]{1,0:T(8,128)(2,1)} async-done(((bf16[288,448]{1,0:T(8,128)(2,1)}), bf16[4608,448]{1,0:T(8,128)(2,1)}) %all-gather.3.cloned.1.call-update) | async-done | bytes 4128784 | tf_op jit(solution)/shard_map/all_gather | solution.py:38
  147.6 6.3 %convolution_multiply_fusion.1 = f32[288,4608]{1,0:T(8,128)} fusion(bf16[288,448]{1,0:T(8,128)(2,1)S(1)} %copy-done.1, bf16[4608,448]{1,0:T(8,128)(2,1)} %all-gather.3.cloned.1.call-done), kind=kOutput, calls=%fused_computation.2 | convolution fusion | flops 1190412288 | bytes 9695232 | tf_op jit(solution)/shard_map/dot_general | solution.py:12
  154.1 223.9 %all-reduce.6.cloned.1.call-done = (f32[288,4608]{1,0:T(8,128)}, f32[288,4608]{1,0:T(8,128)}) async-done(((f32[288,4608]{1,0:T(8,128)}, f32[288,4608]{1,0:T(8,128)}), (f32[288,4608]{1,0:T(8,128)}, f32[288,4608]{1,0:T(8,128)})) %all-reduce.6.cloned.1.call-update) | async-done | bytes 10616848 | tf_op jit(solution)/shard_map/psum | solution.py:44
  378.0 2.9 reduce_max.18
  380.9 3.5 fusion.1
  384.4 0.5 copy-done
  384.9 5.1 select_reduce_fusion
  390.0 0.6 subtract_reduce_fusion
  390.6 1.7 multiply_convert_fusion.1
  392.3 3.3 fusion.24
  395.7 2.7 fusion.26
  398.4 6.9 %maximum_multiply_fusion = f32[4608,896]{1,0:T(8,128)} fusion(f32[4608,448]{1,0:T(8,128)S(1)} %fusion.24, f32[4608,448]{1,0:T(8,128)S(1)} %fusion.26), kind=kLoop, calls=%fused_computation | loop fusion | flops 8257536 | bytes 33030144 | tf_op jit(solution)/shard_map/mul | solution.py:64
  405.4 4.8 fusion.25
  410.1 139.8 %reduce-scatter.2.cloned.1.call-done = f32[288,896]{1,0:T(8,128)} async-done(((f32[4608,896]{1,0:T(8,128)}), f32[288,896]{1,0:T(8,128)}) %reduce-scatter.2.cloned.1.call-update) | async-done | bytes 1032208 | tf_op jit(solution)/shard_map/reduce_scatter | solution.py:63
  549.9 6.2 %fusion.19 = (f32[288]{0:T(512)S(1)}, f32[288]{0:T(512)S(1)}, f32[288,448]{1,0:T(8,128)S(1)}) fusion(bf16[288,448]{1,0:T(8,128)(2,1)S(1)} %copy-done.2, f32[288,896]{1,0:T(8,128)} %reduce-scatter.2.cloned.1.call-done, f32[448]{0:T(512)S(1)} %copy-done.5, bf16[288,448]{1,0:T(8,128)(2,1)S(1)} %copy-done.3, f32[288,448]{1,0:T(8,128)} %fusion.25, ...), kind=kOutput, calls=%fused_computation.34 | convolution fusion | flops 1197139456 | bytes 12024064 | tf_op jit(solution)/shard_map/dot_general | solution.py:61
  556.2 15.3 %all-reduce.1 = (f32[288]{0:T(512)S(1)}, f32[288]{0:T(512)S(1)}) all-reduce(f32[288]{0:T(512)S(1)} %get-tuple-element.10, f32[288]{0:T(512)S(1)} %get-tuple-element.9), channel_id=1, replica_groups=mesh['dp'=16,'tensor'=8] {'tensor'}, use_global_device_ids=true, to_apply=%region_12.13 | all-reduce | flops 576 | bytes 4608 | tf_op jit(solution)/shard_map/psum | solution.py:74
  571.5 1.2 fusion.21
  572.7 37.9 %all-reduce = (f32[448]{0:T(512)}, f32[]{:T(128)}) all-reduce(f32[448]{0:T(512)S(1)} %add.65, f32[]{:T(128)} %get-tuple-element.21), channel_id=1, replica_groups=mesh['dp'=16,'tensor'=8] {'dp'}, use_global_device_ids=true, to_apply=%region_17.18 | all-reduce | flops 449 | bytes 3592 | tf_op jit(solution)/shard_map/psum | solution.py:82
  (31 shorter events, 0.5 us)
Async XLA Ops:
  7.2 81.9 %all-gather.5.cloned.1.call-start = ((), (), s32[]{:S(2)}) async-start(), calls=%async_computation.2 | async-start | bytes 5013504 | tf_op jit(solution)/shard_map/all_gather | solution.py:37
  27.6 120.0 %all-gather.3.cloned.1.call-start = ((), (), s32[]{:S(2)}) async-start(), calls=%async_computation.1 | async-start | bytes 5013504 | tf_op jit(solution)/shard_map/all_gather | solution.py:38
  28.3 119.3 %copy-start.1 = (bf16[288,448]{1,0:T(8,128)(2,1)S(1)}, bf16[288,448]{1,0:T(8,128)(2,1)}, u32[]{:S(2)}) copy-start(bf16[288,448]{1,0:T(8,128)(2,1)} %get-tuple-element.26) | copy-start | bytes 774148
  28.3 349.7 %all-reduce.6.cloned.1.call-start = ((), (), s32[]{:S(2)}) async-start(), calls=%async_computation.4 | async-start | bytes 21233664 | tf_op jit(solution)/shard_map/psum | solution.py:44
  153.9 396.0 %reduce-scatter.2.cloned.1.call-start = ((), (), s32[]{:S(2)}) async-start(), calls=%async_computation.3 | async-start | bytes 17547264 | tf_op jit(solution)/shard_map/reduce_scatter | solution.py:63
  378.0 6.4 %copy-start.6 = (s32[288]{0:T(512)S(1)}, s32[288]{0:T(512)}, u32[]{:S(2)}) copy-start(s32[288]{0:T(512)} %param.7) | copy-start | bytes 3460
  380.9 4.1 copy-start
  380.9 9.8 %slice-start = ((s8[5308416]{0:T(1024)(128)(4,1)}), s8[4194304]{0:T(1024)(128)(4,1)S(1)}, s32[]{:S(2)}) async-start(s8[5308416]{0:T(1024)(128)(4,1)} %bitcast.10), calls=%async_computation.5 | async-start | bytes 8388608
  384.9 5.7 slice-start.1
  405.3 144.6 %copy-start.2 = (bf16[288,448]{1,0:T(8,128)(2,1)S(1)}, bf16[288,448]{1,0:T(8,128)(2,1)}, u32[]{:S(2)}) copy-start(bf16[288,448]{1,0:T(8,128)(2,1)} %param.5) | copy-start | bytes 774148
  405.3 144.6 %copy-start.3 = (bf16[288,448]{1,0:T(8,128)(2,1)S(1)}, bf16[288,448]{1,0:T(8,128)(2,1)}, u32[]{:S(2)}) copy-start(bf16[288,448]{1,0:T(8,128)(2,1)} %param.4) | copy-start | bytes 774148
  405.3 144.6 %copy-start.5 = (f32[448]{0:T(512)S(1)}, f32[448]{0:T(512)}, u32[]{:S(2)}) copy-start(f32[448]{0:T(512)} %param.6) | copy-start | bytes 5380
  549.9 21.6 %copy-start.4 = (f32[288,896]{1,0:T(8,128)S(1)}, f32[288,896]{1,0:T(8,128)}, u32[]{:S(2)}) copy-start(f32[288,896]{1,0:T(8,128)} %reduce-scatter.2.cloned.1.call-done) | copy-start | bytes 3096580
Sparse Core Ops, SparseCore 0:
  27.7 61.3 all-gather.4
  92.1 55.4 all-gather.2
  154.0 223.9 all-reduce.5
  405.4 144.4 reduce-scatter.1
where the time goes:
time: 619 us
  waiting for transfers between devices  477 us (77%)
  blocking collectives  70.1 us (11%)
  matrix products  29.7 us (5%)
  other arithmetic  25.3 us (4%)
  between operations  15.7 us (3%)
    psum x1, waiting for transfers between devices, shards(): logit_d, logit_q = lax.psum((part_d, part_q), 'tensor')  224 us
    reduce_scatter x1, waiting for transfers between devices, shards(): lax.psum_scatter(jnp.concatenate([contract_rows(weight_d, query_emb), con...  140 us
    all_gather x1, waiting for transfers between devices, shards(): lax.all_gather(query_emb, 'dp', axis=0, tiled=True)  60.7 us
    all_gather x1, waiting for transfers between devices, shards(): lax.all_gather(doc_emb, 'dp', axis=0, tiled=True)  52.1 us
    psum x1, blocking collectives, shards(): grad_gain, loss_sum = lax.psum((gain_local, loss_rows), 'dp')  37.9 us
    psum x1, blocking collectives, shards(): lax.psum((jnp.sum(normed_q * normed_q, axis=1), jnp.sum(normed_d * normed...  17 us
    psum x1, blocking collectives, shards(): lax.psum((jnp.sum(grad_emb_q * normed_q, axis=1), jnp.sum(grad_emb_d * no...  15.3 us
    dot_general x2, matrix products, contract_cols(): lax.dot_general(left, right, (((1,), (1,)), ((), ())), preferred_element_...  12.7 us
  transfers between devices with their start and end apart: 4, of which 4 were waited for; matrix products, arithmetic and copies ran while one was open for 2% of the time, Pallas kernels for 0%

commit v1 on v0

v1 whole, which is shorter than its diff:
```python
import jax
import jax.numpy as jnp
from jax import lax
from jax.sharding import PartitionSpec as P

eps_len = 1e-06
inv_temp = 100.0
masked = -1e30


def contract_cols(left, right):
    return lax.dot_general(
        left, right, (((1,), (1,)), ((), ())), preferred_element_type=jnp.float32
    )


def contract_rows(left, right):
    return lax.dot_general(
        left, right, (((0,), (0,)), ((), ())), preferred_element_type=jnp.float32
    )


def shards(query_states, doc_states, gain, positives):
    rows, feats = query_states.shape
    groups = lax.axis_size("dp")
    parts = lax.axis_size("tensor")
    own = lax.axis_index("dp")
    part = lax.axis_index("tensor")
    take = rows // parts
    pairs = rows * groups
    hq = query_states.astype(jnp.float32)
    hd = doc_states.astype(jnp.float32)
    normed_q = hq * gain[None, :]
    normed_d = hd * gain[None, :]
    length_q, length_d = lax.psum(
        (jnp.sum(normed_q * normed_q, axis=1), jnp.sum(normed_d * normed_d, axis=1)), "tensor"
    )
    inverse_q = lax.rsqrt(length_q + eps_len)
    inverse_d = lax.rsqrt(length_d + eps_len)
    query_emb = (normed_q * inverse_q[:, None]).astype(jnp.bfloat16)
    doc_emb = (normed_d * inverse_d[:, None]).astype(jnp.bfloat16)
    query_full = lax.all_gather(query_emb, "tensor", axis=1, tiled=True)
    doc_full = lax.all_gather(doc_emb, "tensor", axis=1, tiled=True)
    subset = lax.dynamic_slice_in_dim(query_full, part * take, take, axis=0)
    query_rows = lax.all_gather(subset, "dp", axis=0, tiled=True)
    row_ids = (
        (lax.iota(jnp.int32, groups) * rows)[:, None]
        + part * take
        + lax.iota(jnp.int32, take)[None, :]
    ).reshape(-1)
    col_ids = own * rows + lax.iota(jnp.int32, rows)
    positive_rows = lax.all_gather(
        lax.dynamic_slice_in_dim(positives, part * take, take, axis=0), "dp", axis=0, tiled=True
    )
    logit_d = contract_cols(query_rows, doc_full) * inv_temp
    logit_q = contract_cols(query_rows, query_full) * inv_temp
    logit_q = jnp.where(row_ids[:, None] == col_ids[None, :], masked, logit_q)
    hit = positive_rows[:, None] == col_ids[None, :]
    top = jnp.maximum(jnp.max(logit_d, axis=1), jnp.max(logit_q, axis=1))
    total = jnp.sum(jnp.exp(logit_d - top[:, None]), axis=1) + jnp.sum(
        jnp.exp(logit_q - top[:, None]), axis=1
    )
    posit = jnp.sum(jnp.where(hit, logit_d, 0.0), axis=1)
    stats = lax.all_gather(jnp.stack([top, total, posit]), "dp", axis=0)
    all_top = jnp.max(stats[:, 0], axis=0)
    lse = all_top + jnp.log(jnp.sum(stats[:, 1] * jnp.exp(stats[:, 0] - all_top[None, :]), axis=0))
    loss_rows = jnp.sum(lse - jnp.sum(stats[:, 2], axis=0))
    lse_cols = lax.all_gather(
        lax.dynamic_slice_in_dim(lse, own * take, take, axis=0), "tensor", axis=0, tiled=True
    )
    weight_d = ((jnp.exp(logit_d - lse[:, None]) - hit.astype(jnp.float32)) / pairs).astype(
        jnp.bfloat16
    )
    weight_q = (jnp.exp(logit_q - lse[:, None]) / pairs).astype(jnp.bfloat16)
    weight_t = (jnp.exp(logit_q - lse_cols[None, :]) / pairs).astype(jnp.bfloat16)
    weight_s = (weight_q.astype(jnp.float32) + weight_t.astype(jnp.float32)).astype(jnp.bfloat16)
    part_q = (
        jnp.dot(weight_d, doc_full, preferred_element_type=jnp.float32)
        + jnp.dot(weight_s, query_full, preferred_element_type=jnp.float32)
    ) * inv_temp
    part_d = contract_rows(weight_d, query_rows) * inv_temp
    back_q = lax.psum_scatter(part_q, "dp", scatter_dimension=0, tiled=True)
    grad_emb_d = lax.psum_scatter(part_d, "tensor", scatter_dimension=1, tiled=True)
    grad_emb_q = lax.all_to_all(back_q, "tensor", split_axis=1, concat_axis=0, tiled=True)
    first_q, first_d = lax.psum(
        (jnp.sum(grad_emb_q * normed_q, axis=1), jnp.sum(grad_emb_d * normed_d, axis=1)), "tensor"
    )
    grad_x_q = inverse_q[:, None] * grad_emb_q - normed_q * (inverse_q**3 * first_q)[:, None]
    grad_x_d = inverse_d[:, None] * grad_emb_d - normed_d * (inverse_d**3 * first_d)[:, None]
    grad_hq = grad_x_q * gain[None, :]
    grad_hd = grad_x_d * gain[None, :]
    gain_local = jnp.sum(grad_x_q * hq, axis=0) + jnp.sum(grad_x_d * hd, axis=0)
    grad_gain = lax.psum(gain_local, "dp")
    loss_sum = lax.psum(loss_rows, "tensor")
    return (grad_hq.astype(jnp.bfloat16), grad_hd.astype(jnp.bfloat16), grad_gain, loss_sum / pairs)


def solution(mesh):
    return jax.shard_map(
        shards,
        mesh=mesh,
        in_specs=(P("dp", "tensor"), P("dp", "tensor"), P("tensor"), P("dp")),
        out_specs=(P("dp", "tensor"), P("dp", "tensor"), P("tensor"), P()),
        check_vma=False,
    )
```

time: 619 us -> 441 us (0.71); the launches traced: 619 us -> 434 us
  waiting for transfers between devices: 477 us -> 121 us
  blocking collectives: 70.1 us -> 222 us
  local copies, waits for them, and re-layouts: 0.58 us -> 39.7 us
  other arithmetic: 25.3 us -> 6.02 us
    psum x1 -> x0, waiting for transfers between devices: 224 us -> none  [shards(): logit_d, logit_q = lax.psum((part_d, part_q), 'tensor')]
    reduce_scatter x1 -> x0, waiting for transfers between devices: 140 us -> none  [shards(): lax.psum_scatter(jnp.concatenate([contract_rows(weight_d, query_emb), con...]
    unnamed x0 -> x3, blocking collectives: none -> 117 us
    unnamed x18 -> x31, local copies, waits for them, and re-layouts: 0.58 us -> 30.1 us
    all_gather x0 -> x1, blocking collectives: none -> 20.4 us  [shards(): stats = lax.all_gather(jnp.stack([top, total, posit]), 'dp', axis=0)]
    all_to_all x0 -> x1, blocking collectives: none -> 14.1 us  [shards(): lax.all_to_all(back_q, 'tensor', split_axis=1, concat_axis=0, tiled=True)]
    unnamed x4 -> x7, waiting for transfers between devices: 0.75 us -> 12.8 us
    all_gather x0 -> x2, local copies, waits for them, and re-layouts: none -> 8.87 us  [the longest x1 4.43 us: shards(): query_full = lax.all_gather(query_emb, 'tensor', axis=1, tiled=True)]
  transfers between devices with their start and end apart: 4 -> 6, of which waited for: 4 -> 4; matrix products, arithmetic and copies ran while one was open for 2% -> 27% of each run, Pallas kernels for 0% -> 0%
where the time goes in v1:
time: 441 us; the launch traced here: 434 us
  blocking collectives  222 us (50%)
  waiting for transfers between devices  121 us (27%)
  local copies, waits for them, and re-layouts  39.7 us (9%)
  matrix products  25 us (6%)
  between operations  17.8 us (4%)
  other arithmetic  6.02 us (1%)
    unnamed x3, blocking collectives  117 us
    all_gather x1, waiting for transfers between devices, shards(): query_rows = lax.all_gather(subset, 'dp', axis=0, tiled=True)  55 us
    all_gather x1, waiting for transfers between devices, shards(): query_full = lax.all_gather(query_emb, 'tensor', axis=1, tiled=True)  39.5 us
    psum x1, blocking collectives, shards(): grad_gain = lax.psum(gain_local, 'dp')  38 us
    unnamed x31, local copies, waits for them, and re-layouts  30.1 us
    all_gather x1, blocking collectives, shards(): stats = lax.all_gather(jnp.stack([top, total, posit]), 'dp', axis=0)  20.4 us
    psum x1, blocking collectives, shards(): lax.psum((jnp.sum(normed_q * normed_q, axis=1), jnp.sum(normed_d * normed...  17 us
    psum x1, blocking collectives, shards(): lax.psum((jnp.sum(grad_emb_q * normed_q, axis=1), jnp.sum(grad_emb_d * no...  15.2 us
  transfers between devices with their start and end apart: 6, of which 4 were waited for; matrix products, arithmetic and copies ran while one was open for 27% of the time, Pallas kernels for 0%

profile of v1, /device:TPU:1, one launch (start us, length us, event | category | flops | bytes accessed | tf_op | source)
XLA Modules:
  0.0 434.4 jit_solution(4988067023685988842)
XLA Ops:
  8.5 17.0 %all-reduce.5 = (f32[288]{0:T(512)S(1)}, f32[288]{0:T(512)S(1)}) all-reduce(f32[288]{0:T(512)S(1)} %get-tuple-element.14, f32[288]{0:T(512)S(1)} %get-tuple-element.13), channel_id=1, replica_groups=mesh['dp'=16,'tensor'=8] {'tensor'}, use_global_device_ids=true, to_apply=%region_3.0 | all-reduce | flops 576 | bytes 4608 | tf_op jit(solution)/shard_map/psum | solution.py:35
  25.5 2.0 fusion.28
  28.4 39.5 %all-gather.9.cloned.1.call-done = bf16[8,448,288]{1,2,0:T(8,128)(2,1)} async-done(((bf16[1,448,288]{1,2,0:T(8,128)(2,1)}), bf16[8,448,288]{1,2,0:T(8,128)(2,1)}) %all-gather.9.cloned.1.call-update) | async-done | bytes 2064400 | tf_op jit(solution)/shard_map/all_gather | solution.py:42
  67.9 4.4 %copy.14 = bf16[8,448,288]{1,0,2:T(8,128)(2,1)} copy(bf16[8,448,288]{1,2,0:T(8,128)(2,1)} %all-gather.9.cloned.1.call-done) | data formatting | bytes 4128768 | tf_op jit(solution)/shard_map/all_gather | solution.py:42
  72.3 4.2 reshape.86
  81.1 17.2 %all-reduce = s32[576]{0:T(1024)S(1)} all-reduce(s32[576]{0:T(1024)S(1)} %dynamic-slice_dynamic-update-slice_fusion.1), channel_id=1, replica_groups=mesh['dp'=16,'tensor'=8] {'dp'}, use_global_device_ids=true, to_apply=%add | all-reduce | flops 576 | bytes 4608
  98.3 13.3 %all-gather.13.cloned.1.call-done = bf16[8,448,288]{1,2,0:T(8,128)(2,1)} async-done(((bf16[1,448,288]{1,2,0:T(8,128)(2,1)}), bf16[8,448,288]{1,2,0:T(8,128)(2,1)}) %all-gather.13.cloned.1.call-update) | async-done | bytes 2064400 | tf_op jit(solution)/shard_map/all_gather | solution.py:43
  111.6 4.4 %copy.15 = bf16[8,448,288]{1,0,2:T(8,128)(2,1)} copy(bf16[8,448,288]{1,2,0:T(8,128)(2,1)} %all-gather.13.cloned.1.call-done) | data formatting | bytes 4128768 | tf_op jit(solution)/shard_map/all_gather | solution.py:43
  116.0 5.2 %reshape.90 = bf16[3584,288]{0,1:T(8,128)(2,1)} reshape(bf16[8,448,288]{1,0,2:T(8,128)(2,1)} %copy.15) | data formatting | bytes 4128768
  121.2 55.0 %all-gather.11.cloned.1.call-done = bf16[16,36,3584]{2,1,0:T(8,128)(2,1)} async-done(((bf16[1,36,3584]{2,1,0:T(8,128)(2,1)}), bf16[16,36,3584]{2,1,0:T(8,128)(2,1)}) %all-gather.11.cloned.1.call-update) | async-done | bytes 4128784 | tf_op jit(solution)/shard_map/all_gather | solution.py:45
  176.2 7.0 %reshape.88 = bf16[576,3584]{1,0:T(8,128)(2,1)} reshape(bf16[16,36,3584]{2,1,0:T(8,128)(2,1)} %all-gather.11.cloned.1.call-done) | data formatting | bytes 8257536
  183.2 4.8 %fusion.41 = (f32[576]{0:T(1024)S(1)}, f32[576,288]{0,1:T(8,128)S(1)}) fusion(bf16[576,3584]{1,0:T(8,128)(2,1)} %reshape.88, bf16[3584,288]{0,1:T(8,128)(2,1)} %reshape.90), kind=kOutput, calls=%fused_computation.72 | convolution fusion | flops 1189416448 | bytes 6859008 | tf_op jit(solution)/shard_map/dot_general | solution.py:12
  190.2 20.4 %all-gather.4 = f32[16,3,576]{2,1,0:T(4,128)S(1)} all-gather(f32[1,3,576]{2,1,0:T(4,128)S(1)} %maximum_bitcast_fusion), channel_id=2, replica_groups=mesh['dp'=16,'tensor'=8] {'dp'}, dimensions={0}, use_global_device_ids=true | all-gather | bytes 117504 | tf_op jit(solution)/shard_map/all_gather | solution.py:64
  211.3 3.8 convolution_multiply_fusion
  215.1 5.6 %fusion.37 = f32[576,3584]{1,0:T(8,128)} fusion(bf16[3584,288]{0,1:T(8,128)(2,1)S(1)} %copy-done, f32[576,288]{0,1:T(8,128)S(1)} %get-tuple-element.33, f32[576]{0:T(1024)S(1)} %get-tuple-element.21, s32[576]{0:T(1024)S(1)} %all-reduce, s32[288]{0:T(512)S(1)} %iota_add_fusion.1), kind=kOutput, calls=%fused_computation.69 | convolution fusion | flops 1190080512 | bytes 10991232 | tf_op jit(solution)/shard_map/dot_general | solution.py:78
  220.7 5.8 %copy.18 = f32[288,3584]{0,1:T(8,128)} copy(f32[288,3584]{1,0:T(8,128)} %convolution_multiply_fusion) | data formatting | bytes 8257536
  226.8 16.7 %all-reduce.1 = f32[288]{0:T(512)S(1)} all-reduce(f32[288]{0:T(512)S(1)} %dynamic-slice_dynamic-update-slice_fusion), channel_id=1, replica_groups=mesh['dp'=16,'tensor'=8] {'tensor'}, use_global_device_ids=true, to_apply=%add.1 | all-reduce | flops 288 | bytes 2304
  243.5 9.1 %add_multiply_fusion = f32[576,3584]{1,0:T(8,128)} fusion(f32[576,3584]{1,0:T(8,128)} %fusion.37, bf16[3584,288]{0,1:T(8,128)(2,1)S(1)} %reshape.86, f32[576,288]{0,1:T(8,128)S(1)} %get-tuple-element.35, f32[288]{0:T(512)S(1)} %all-reduce.1, f32[576]{0:T(1024)S(1)} %get-tuple-element.21), kind=kOutput, calls=%fused_computation | convolution fusion | flops 1194872832 | bytes 19246464 | tf_op jit(solution)/shard_map/dot_general | solution.py:79
  252.6 83.2 %fusion = f32[40,3584]{1,0:T(8,128)S(1)} fusion(f32[576,3584]{1,0:T(8,128)} %add_multiply_fusion), kind=kCustom, calls=%all-reduce-scatter | all-reduce-scatter fusion | flops 2293761 | bytes 8831488
  339.8 12.0 %collective-permute-done.1 = f32[20,3584]{1,0:T(8,128)S(1)} collective-permute-done((f32[20,3584]{1,0:T(8,128)S(1)}, f32[20,3584]{1,0:T(8,128)S(1)}, u32[]{:S(2)}, u32[]{:S(2)}) %collective-permute-start.1) | collective-permute-done | bytes 286752
  352.5 2.6 concatenate
  355.8 14.1 %all_to_all.19 = f32[36,8,448]{2,0,1:T(8,128)S(1)} all-to-all(f32[36,8,448]{2,0,1:T(8,128)S(1)} %copy.17), channel_id=1, replica_groups=mesh['dp'=16,'tensor'=8] {'tensor'}, dimensions={1} | all-to-all | bytes 1032192 | tf_op jit(solution)/shard_map/all_to_all | solution.py:84
  371.6 15.2 %all-reduce.4 = (f32[288]{0:T(512)S(1)}, f32[288]{0:T(512)S(1)}, f32[]{:T(128)}) all-reduce(f32[288]{0:T(512)S(1)} %get-tuple-element.12, f32[288]{0:T(512)S(1)} %get-tuple-element.11, f32[]{:T(128)} %get-tuple-element.20), channel_id=1, replica_groups=mesh['dp'=16,'tensor'=8] {'tensor'}, use_global_device_ids=true, to_apply=%region_13.14 | all-reduce | flops 577 | bytes 4616 | tf_op jit(solution)/shard_map/psum | solution.py:85
  388.0 38.0 %psum.46 = f32[448]{0:T(512)} all-reduce(f32[448]{0:T(512)S(1)} %add.116), channel_id=1, replica_groups=mesh['dp'=16,'tensor'=8] {'dp'}, use_global_device_ids=true, to_apply=%region_19.20 | all-reduce | flops 448 | bytes 3584 | tf_op jit(solution)/shard_map/psum | solution.py:93
  (63 shorter events, 16.0 us)
Async XLA Ops:
  7.2 60.7 %all-gather.9.cloned.1.call-start = ((), (), s32[]{:S(2)}) async-start(), calls=%async_computation.2 | async-start | bytes 2654208 | tf_op jit(solution)/shard_map/all_gather | solution.py:42
  27.6 84.0 %all-gather.13.cloned.1.call-start = ((), (), s32[]{:S(2)}) async-start(), calls=%async_computation.4 | async-start | bytes 2654208 | tf_op jit(solution)/shard_map/all_gather | solution.py:43
  28.3 147.9 %all-gather.11.cloned.1.call-start = ((), (), s32[]{:S(2)}) async-start(), calls=%async_computation.3 | async-start | bytes 4874240 | tf_op jit(solution)/shard_map/all_gather | solution.py:45
  28.4 49.2 %copy-start.7 = (u32[128]{0:T(128)S(1)}, u32[128]{0:T(128)}, u32[]{:S(2)}) copy-start(u32[128]{0:T(128)} %constant.44) | copy-start | bytes 1540
  28.4 49.9 %copy-start.6 = (u32[128]{0:T(128)S(1)}, u32[128]{0:T(128)}, u32[]{:S(2)}) copy-start(u32[128]{0:T(128)} %constant.39) | copy-start | bytes 1540
  77.4 292.6 %reduce-scatter.6.cloned.1.call-start = ((), (), s32[]{:S(2)}) async-start(), calls=%async_computation.5 | async-start | bytes 6193152
  183.2 4.8 %copy-start.3 = (bf16[576,3584]{1,0:T(8,128)(2,1)S(1)}, bf16[576,3584]{1,0:T(8,128)(2,1)}, u32[]{:S(2)}) copy-start(bf16[576,3584]{1,0:T(8,128)(2,1)} %reshape.88) | copy-start | bytes 12386308
  211.3 3.8 copy-start
  335.8 16.6 %collective-permute-start = (f32[40,3584]{1,0:T(8,128)S(1)}, f32[40,3584]{1,0:T(8,128)S(1)}, u32[]{:S(2)}, u32[]{:S(2)}) collective-permute-start(f32[40,3584]{1,0:T(8,128)S(1)} %fusion), channel_id=1, source_target_pairs={{0,8},{8,16},{16,24},{24,32},{32,40},{40,48},{48,56},{56,64},{64,7... | collective-permute-start | bytes 1720328
  337.8 14.0 %collective-permute-start.1 = (f32[20,3584]{1,0:T(8,128)S(1)}, f32[20,3584]{1,0:T(8,128)S(1)}, u32[]{:S(2)}, u32[]{:S(2)}) collective-permute-start(f32[20,3584]{1,0:T(8,128)S(1)} %slice.16), channel_id=1, source_target_pairs={{0,16},{8,24},{16,32},{24,40},{32,48},{40,56},{48,64},{56,72},{64,... | collective-permute-start | bytes 860168
  351.8 0.7 copy-start.4
  355.0 16.3 %copy-start.1 = (bf16[288,448]{1,0:T(8,128)(2,1)S(1)}, bf16[288,448]{1,0:T(8,128)(2,1)}, u32[]{:S(2)}) copy-start(bf16[288,448]{1,0:T(8,128)(2,1)} %param.5) | copy-start | bytes 774148
  355.1 16.3 %copy-start.2 = (bf16[288,448]{1,0:T(8,128)(2,1)S(1)}, bf16[288,448]{1,0:T(8,128)(2,1)}, u32[]{:S(2)}) copy-start(bf16[288,448]{1,0:T(8,128)(2,1)} %param.4) | copy-start | bytes 774148
  355.1 16.3 %copy-start.5 = (f32[448]{0:T(512)S(1)}, f32[448]{0:T(512)}, u32[]{:S(2)}) copy-start(f32[448]{0:T(512)} %param.6) | copy-start | bytes 5380
Sparse Core Ops, SparseCore 0:
  27.7 40.1 all-gather.8
  70.1 41.4 all-gather.12
  114.6 61.5 all-gather.10
  226.7 78.7 reduce-scatter.5

commit v2 on v0

v2 whole, which is shorter than its diff:
```python
import functools

import jax
import jax.numpy as jnp
from jax import lax
from jax.experimental import pallas as pl
from jax.experimental.pallas import tpu as pltpu
from jax.sharding import PartitionSpec as P

eps_len = 1e-06
inv_temp = 100.0
masked = -1e30

MESH = pl.DeviceIdType.MESH
HIGH = lax.Precision.HIGHEST
f32 = jnp.float32
bf16 = jnp.bfloat16

DP = 16
TP = 8
ROWS = 288
FEATS = 448
WIDE = 2 * FEATS
FULL = TP * FEATS
PAIRS = DP * ROWS
TAKE = DP * ROWS // TP
TILE = 16
CHUNK = 96
NCH = ROWS // CHUNK
HALF = CHUNK // 2


def step(
    hq, hd, gain, pos,
    oq, od, ogain, oloss,
    xq, xd, pq, pd, gpart, emb, qi, invq, invd, logits, wts, wtt,
    e0s, e0r, cs1, cr1, e1s, e1r, e2s, e2r, e3s, e3r, cs4, cr4, e4s, e4r, epr,
    partq, sibr, sendq, recvq, pd2, pd1, pdm, halfs, r1, r2, gd, xsend, xrecv,
    asend, arecv, gqs, outq, outd,
    x_s, x_r, e0_s, e0_r, e1_s, e1_r, e2_s, e2_r, e3_s, e3_r, e4_s, e4_r, ep_s, ep_r,
    y_s, y_r, a_s, a_r, loc, b_s, b_r, u_s, u_r, g_s, g_r, t_s, t_r, c_s, c_r, io,
):
    d = lax.axis_index("dp")
    t = lax.axis_index("tensor")
    hz = d // 2
    core = d % 2
    zc = hz % 4
    d4 = (hz // 4) * 2 + core
    low = t // 4
    y = t % 4
    xh = hz // 4
    sources = [pltpu.make_async_copy(hq, xq, io.at[0]), pltpu.make_async_copy(hd, xd, io.at[1])]
    for c in sources:
        c.start()
    third = t // 2
    sibling = (hz * 2 + (1 - core), t)
    partner = (d, (t + 4) % TP)
    up = (d, low * 4 + (y + 1) % 4)
    down = (d, low * 4 + (y + 3) % 4)
    zup = ((xh * 4 + (zc + 1) % 4) * 2 + core, t)
    zdown = ((xh * 4 + (zc + 3) % 4) * 2 + core, t)
    across = ((hz + 4) % 8 * 2 + core, t)

    sent = []

    def copy(src, dst, ss, rs, dev):
        return pltpu.make_async_remote_copy(
            src_ref=src, dst_ref=dst, send_sem=ss, recv_sem=rs, device_id=dev, device_id_type=MESH
        )

    def lanes(block):
        return pl.ds(pl.multiple_of(block * WIDE, 128), WIDE)

    def rows_at(tile, n):
        return pl.ds(pl.multiple_of(tile * TILE, TILE), n)

    def place(hz_s, core_s, tens):
        q = (hz_s // 4) * 2 + core_s
        e = tens // 2
        return (hz_s % 4) * 9 + 2 * q + jnp.where(q > e, 1, 0)

    def begin(q, tens):
        return 2 * tens + jnp.clip(tens - 2 * q, 0, 2)

    def sized(extra, fn):
        @pl.when(extra)
        def _():
            fn(3 * TILE)

        @pl.when(jnp.logical_not(extra))
        def _():
            fn(2 * TILE)

    barrier = pltpu.get_barrier_semaphore()

    @pl.loop(1, TP)
    def _(k):
        pl.semaphore_signal(barrier, inc=1, device_id=(d, (t + k) % TP), device_id_type=MESH)

    @pl.loop(1, 8)
    def _(k):
        pl.semaphore_signal(
            barrier, inc=1, device_id=((hz + k) % 8 * 2 + core, t), device_id_type=MESH
        )

    pl.semaphore_signal(barrier, inc=1, device_id=sibling, device_id_type=MESH)
    def to_lanes(col):
        return jnp.transpose(jnp.broadcast_to(col, (ROWS, 128)))[:8]

    def to_rows(vec):
        return jnp.transpose(jnp.broadcast_to(vec, (128, ROWS)))

    sub8 = lambda n: lax.broadcasted_iota(jnp.int32, (8, n), 0)

    for c in sources:
        c.wait()
    nq = xq[...].astype(f32) * gain[...]
    nd = xd[...].astype(f32) * gain[...]
    lq = to_lanes(jnp.sum(nq * nq, axis=1, keepdims=True))
    ld = to_lanes(jnp.sum(nd * nd, axis=1, keepdims=True))
    e0s[...] = jnp.where(sub8(ROWS) == 0, lq, ld)
    pl.semaphore_wait(barrier, TP + 7)

    def xcopy(i):
        if i == 0:
            return copy(gain, gpart, x_s.at[0], x_r.at[0], partner)
        src, dst = (xq, pq) if i <= NCH else (xd, pd)
        part = pl.ds(((i - 1) % NCH) * CHUNK, CHUNK)
        return copy(src.at[part], dst.at[part], x_s.at[i], x_r.at[i], partner)

    def begun(c):
        c.start()
        sent.append(c.wait_send)

    def exchange(src, recv, ss, rs, size, me, dev):
        @pl.loop(1, size)
        def _(k):
            copy(src, recv.at[me], ss.at[k], rs.at[me], dev((me + k) % size)).start()

        @sent.append
        def _():
            @pl.loop(1, size)
            def _(k):
                copy(src, recv.at[me], ss.at[k], rs.at[me], dev((me + k) % size)).wait_send()

    def finish(src, recv, ss, rs, size, me, dev):
        recv[me] = src[...]

        @pl.loop(1, size)
        def _(k):
            s = (me + k) % size
            copy(src, recv.at[s], ss.at[k], rs.at[s], dev(s)).wait_recv()

    by_tensor = lambda s: (d, s)
    by_hz = lambda s: (s * 2 + core, t)

    def total(recv, size):
        acc = recv[0]
        for s in range(1, size):
            acc = acc + recv[s]
        return acc

    e0 = (e0s, e0r, e0_s, e0_r, TP, t, by_tensor)
    begun(xcopy(0))
    begun(xcopy(1))
    exchange(*e0)
    for i in range(2, 1 + 2 * NCH):
        begun(xcopy(i))

    mine = begin(d4, t)
    here = place(hz, core, t)
    extra = d4 == third

    finish(*e0)
    inv = lax.rsqrt(total(e0r, TP) + eps_len)
    invq[0:ROWS] = to_rows(inv[0:1])
    invd[...] = to_rows(inv[1:2])

    def pack(a, k):
        own, part, inverse, base = (xq, pq, invq, ROWS) if a == 0 else (xd, pd, invd, 0)
        xcopy(1 + a * NCH + k).wait_recv()
        rs = pl.ds(k * CHUNK, CHUNK)
        scale = inverse[rs, 0:1]
        eo = own[rs].astype(f32) * gain[...] * scale
        ep = part[rs].astype(f32) * gpart[...] * scale
        left = jnp.where(low == 0, eo, ep)
        right = jnp.where(low == 0, ep, eo)
        emb[pl.ds(base + k * CHUNK, CHUNK), lanes(y)] = jnp.concatenate(
            [left, right], axis=1
        ).astype(bf16)

    def ycopy(a, k, kind):
        base = (ROWS if a == 0 else 0) + k * CHUNK
        i = (a * NCH + k) * 4 + kind
        if kind < 2:
            at, dev, block = pl.ds(base, CHUNK), (up, down)[kind], y
        elif kind == 2:
            at, dev, block = pl.ds(base, HALF), up, (y + 3) % 4
        else:
            at, dev, block = pl.ds(base + HALF, HALF), down, (y + 1) % 4
        ref = emb.at[at, lanes(block)]
        return copy(ref, ref, y_s.at[i], y_r.at[i], dev)

    def yrecv(a, k, kind):
        base = (ROWS if a == 0 else 0) + k * CHUNK
        i = (a * NCH + k) * 4 + kind
        at = pl.ds(base, CHUNK) if kind < 2 else pl.ds(base + (kind - 2) * HALF, HALF)
        block = ((y + 3) % 4, (y + 1) % 4, (y + 2) % 4, (y + 2) % 4)[kind]
        ref = emb.at[at, lanes(block)]
        copy(ref, ref, y_s.at[i], y_r.at[i], up).wait_recv()

    def arow(i, hz_s, core_s, n):
        block = (y + (0, 3, 1, 2)[i]) % 4
        return qi.at[rows_at(place(hz_s, core_s, t), n), lanes(block)]

    def own_rows(i, n):
        block = (y + (0, 3, 1, 2)[i]) % 4
        return emb.at[pl.ds(pl.multiple_of(ROWS + mine * TILE, TILE), n), lanes(block)]

    def acopy(i, k, n):
        to = (hz + k) % 8 * 2 + jnp.where(k == 0, 1 - core, core)
        return copy(
            own_rows(i, n), arow(i, hz, core, n), a_s.at[i * 16 + k], a_r.at[i * 16 + k], (to, t)
        )

    def alocal(i, n):
        return pltpu.make_async_copy(own_rows(i, n), arow(i, hz, core, n), loc.at[i])

    def arrived(i, k, core_s, slot, n):
        ref = arow(i, (hz + 8 - k) % 8, core_s, n)
        return copy(ref, ref, a_s.at[i * 16 + slot], a_r.at[i * 16 + slot], sibling)

    def gives(k, core_s):
        return (((hz + 8 - k) % 8) // 4) * 2 + core_s == third

    def astart(i):
        @pl.loop(0, 8)
        def _(k):
            sized(extra, lambda n: acopy(i, k, n).start())

        sized(extra, lambda n: alocal(i, n).start())

        @sent.append
        def _():
            @pl.loop(0, 8)
            def _(k):
                sized(extra, lambda n: acopy(i, k, n).wait_send())

    def aforward(i):
        @pl.loop(1, 8)
        def _(k):
            def pass_on(n):
                arrived(i, k, core, k, n).wait_recv()
                arrived(i, k, core, 8 + k, n).start()

            sized(gives(k, core), pass_on)

        @sent.append
        def _():
            @pl.loop(1, 8)
            def _(k):
                sized(gives(k, core), lambda n: arrived(i, k, core, 8 + k, n).wait_send())

    def afinish(i):
        sized(extra, lambda n: alocal(i, n).wait())
        sized(gives(0, 1 - core), lambda n: arrived(i, 0, 1 - core, 0, n).wait_recv())

        @pl.loop(1, 8)
        def _(k):
            sized(gives(k, 1 - core), lambda n: arrived(i, k, 1 - core, 8 + k, n).wait_recv())

    xcopy(0).wait_recv()
    for k in range(NCH):
        pack(0, k)
        begun(ycopy(0, k, 0))
        begun(ycopy(0, k, 1))
    astart(0)
    ep = (pos, epr, ep_s, ep_r, 8, hz, by_hz)
    exchange(*ep)
    for k in range(NCH):
        yrecv(0, k, 0)
        begun(ycopy(0, k, 2))
        yrecv(0, k, 1)
        begun(ycopy(0, k, 3))
        pack(1, k)
        begun(ycopy(1, k, 0))
        begun(ycopy(1, k, 1))
    astart(1)
    astart(2)
    aforward(0)
    for k in range(NCH):
        yrecv(0, k, 2)
        yrecv(0, k, 3)
    astart(3)
    aforward(1)
    aforward(2)
    for k in range(NCH):
        yrecv(1, k, 0)
        begun(ycopy(1, k, 2))
        yrecv(1, k, 1)
        begun(ycopy(1, k, 3))
    aforward(3)
    for i in range(4):
        afinish(i)

    lane_p = lax.broadcasted_iota(jnp.int32, (1, TAKE), 1)
    tile_p = lane_p // TILE
    w_p = tile_p % 9
    q_p = jnp.where(
        w_p < 2 * third, w_p // 2, jnp.where(w_p <= 2 * third + 2, third, (w_p - 1) // 2)
    )
    off_p = w_p - 2 * q_p - jnp.where(q_p > third, 1, 0)
    dev_p = (q_p // 2) * 8 + (tile_p // 9) * 2 + q_p % 2
    row_p = dev_p * ROWS + (begin(q_p, t) + off_p) * TILE + lane_p % TILE
    finish(*ep)
    epc = copy(epr.at[pl.ds(0, 8)], epr.at[pl.ds(8, 8)], c_s.at[0], c_r.at[0], sibling)
    begun(epc)

    MC = 144

    def logit_rows(r, query):
        at = pl.ds(pl.multiple_of(r, TILE), MC)
        s = lax.dot_general(
            emb[at], qi[...], (((1,), (1,)), ((), ())), preferred_element_type=f32
        ) * inv_temp
        if query:
            j = d * ROWS + r - ROWS + lax.broadcasted_iota(jnp.int32, (MC, TAKE), 0)
            s = jnp.where(j == row_p, masked, s)
        logits[at] = s

    @pl.loop(0, ROWS // MC)
    def _(m):
        logit_rows(ROWS + m * MC, True)

    epc.wait_recv()
    local_p = (begin(q_p, t) + off_p) * TILE + lane_p % TILE
    lane_of = lax.broadcasted_iota(jnp.int32, (128, TAKE), 0)
    spread = jnp.where(lane_of == local_p % 128, 1.0, 0.0).astype(bf16)
    found = jnp.dot(
        epr[...].reshape(DP * 8, 128).astype(bf16), spread, preferred_element_type=f32
    )
    slot_p = jnp.where(dev_p % 2 == core, dev_p // 2, 8 + dev_p // 2) * 8 + local_p // 128
    high = jnp.sum(jnp.where(lane_of == slot_p, found, 0.0), axis=0, keepdims=True)
    rest = jnp.sum(jnp.where(lane_of == slot_p + 3, found, 0.0), axis=0, keepdims=True)
    pos_p = (high * 128.0 + rest).astype(jnp.int32)

    for k in range(NCH):
        yrecv(1, k, 2)
        yrecv(1, k, 3)

    @pl.loop(0, ROWS // MC)
    def _(m):
        logit_rows(m * MC, False)

    own_j = d * ROWS + lax.broadcasted_iota(jnp.int32, (ROWS, TAKE), 0)
    top = jnp.max(logits[...], axis=0, keepdims=True)
    tot = jnp.sum(jnp.exp(logits[...] - top), axis=0, keepdims=True)
    posit = jnp.sum(
        jnp.where(own_j == pos_p, logits[0:ROWS], 0.0), axis=0, keepdims=True
    )
    sub_t = sub8(TAKE)
    cs1[...] = jnp.where(sub_t == 0, top, jnp.where(sub_t == 1, tot, posit))
    c1 = copy(cs1, cr1, c_s.at[1], c_r.at[1], sibling)
    begun(c1)
    c1.wait_recv()
    top_o = cr1[0:1]
    top_c = jnp.maximum(top, top_o)
    tot = tot * jnp.exp(top - top_c) + cr1[1:2] * jnp.exp(top_o - top_c)
    e1s[...] = jnp.where(sub_t == 0, top_c, jnp.where(sub_t == 1, tot, posit + cr1[2:3]))
    e1 = (e1s, e1r, e1_s, e1_r, 8, hz, by_hz)
    exchange(*e1)
    finish(*e1)
    all_top = e1r[0, 0:1]
    for s in range(1, 8):
        all_top = jnp.maximum(all_top, e1r[s, 0:1])
    all_tot = jnp.zeros_like(all_top)
    all_pos = jnp.zeros_like(all_top)
    for s in range(8):
        all_tot = all_tot + e1r[s, 1:2] * jnp.exp(e1r[s, 0:1] - all_top)
        all_pos = all_pos + e1r[s, 2:3]
    lse = all_top + jnp.log(all_tot)
    loss_part = jnp.sum(lse - all_pos, axis=1, keepdims=True)

    pick = (own_j == row_p).astype(f32)
    lse_own = lax.dot_general(
        jnp.broadcast_to(lse, (8, TAKE)), pick, (((1,), (1,)), ((), ())),
        precision=HIGH, preferred_element_type=f32,
    )
    e2s[...] = jnp.where(sub8(ROWS) == 0, lse_own, loss_part)
    e2 = (e2s, e2r, e2_s, e2_r, TP, t, by_tensor)
    exchange(*e2)
    wd = (jnp.exp(logits[0:ROWS] - lse) - (own_j == pos_p).astype(f32)) * (1.0 / PAIRS)
    wts[0:ROWS] = wd.astype(bf16)

    def part_d(block):
        return lax.dot_general(
            wts[0:ROWS], qi[:, lanes(block)], (((1,), (0,)), ((), ())),
            preferred_element_type=f32,
        ) * inv_temp

    MID = ROWS // 2
    pd2[...] = part_d((y + 2) % 4).astype(bf16)
    gc = [
        copy(pd2.at[pl.ds(0, MID)], halfs.at[0], g_s.at[0], g_r.at[0], up),
        copy(pd2.at[pl.ds(MID, MID)], halfs.at[1], g_s.at[1], g_r.at[1], down),
        copy(pd1, r1, g_s.at[2], g_r.at[2], up),
        copy(pdm, r2, g_s.at[3], g_r.at[3], down),
        copy(xsend, xrecv, g_s.at[4], g_r.at[4], partner),
    ]
    begun(gc[0])
    begun(gc[1])

    finish(*e2)
    sums = total(e2r, TP)
    oloss[...] = sums[1:2, 0:1] * (1.0 / PAIRS)
    lse_j = to_rows(sums[0:1])[:, 0:1]
    wq = (jnp.exp(logits[ROWS:] - lse) * (1.0 / PAIRS)).astype(bf16).astype(f32)
    wt = (jnp.exp(logits[ROWS:] - lse_j) * (1.0 / PAIRS)).astype(bf16).astype(f32)
    wts[ROWS:] = (wq + wt).astype(bf16)
    wtt[...] = jnp.transpose(wts[...])

    def target(s):
        return (xh + s // 4) % 2 * 4 + (zc + s % 4) % 4

    def bcopy(f, k, n):
        at = rows_at(place(k, 1 - core, t), n)
        return copy(
            partq.at[at, pl.ds(f * WIDE, WIDE)], sibr.at[k, pl.ds(0, n), pl.ds(f * WIDE, WIDE)],
            b_s.at[f * 8 + k], b_r.at[f * 8 + k], sibling,
        )

    def three(k, core_s):
        return (k // 4) * 2 + core_s == third

    def part_q(f):
        partq[0:TAKE, f * WIDE : (f + 1) * WIDE] = (
            jnp.dot(
                wtt[...], emb[0 : 2 * ROWS, f * WIDE : (f + 1) * WIDE],
                preferred_element_type=f32,
            ) * inv_temp
        ).astype(bf16)

        @pl.loop(0, 8)
        def _(k):
            sized(three(k, 1 - core), lambda n: bcopy(f, k, n).start())

        @sent.append
        def _():
            @pl.loop(0, 8)
            def _(k):
                sized(three(k, 1 - core), lambda n: bcopy(f, k, n).wait_send())

    N3 = 3 * TILE

    def both(f, s):
        k = target(s)
        sized(three(k, core), lambda n: bcopy(f, k, n).wait_recv())
        cs = slice(f * WIDE, (f + 1) * WIDE)
        return partq[rows_at(place(k, core, t), N3), cs].astype(f32) + sibr[k, :, cs].astype(f32)

    FLOW = ((2, zup), (6, zdown), (5, zup), (3, zdown), (1, zup), (7, zdown), (4, across))

    def ucopy(f, i, n):
        cs = pl.ds(f * WIDE, WIDE)
        return copy(
            sendq.at[i, pl.ds(0, n), cs], recvq.at[i, pl.ds(0, n), cs],
            u_s.at[f * 8 + i], u_r.at[f * 8 + i], FLOW[i][1],
        )

    def usend(f, i, value):
        sendq[i, :, f * WIDE : (f + 1) * WIDE] = value.astype(bf16)
        far = three(target(FLOW[i][0]), core)
        sized(far, lambda n: ucopy(f, i, n).start())
        sent.append(lambda: sized(far, lambda n: ucopy(f, i, n).wait_send()))

    def uwait(f, i, s):
        sized(three(target(s), core), lambda n: ucopy(f, i, n).wait_recv())
        return recvq[i, :, f * WIDE : (f + 1) * WIDE].astype(f32)

    def q_far(f):
        usend(f, 0, both(f, 2))
        usend(f, 1, both(f, 6))
        usend(f, 2, both(f, 5))
        usend(f, 3, both(f, 3))

    def q_near(f):
        usend(f, 4, both(f, 1) + uwait(f, 0, 1))
        usend(f, 5, both(f, 7) + uwait(f, 1, 7))

    def q_across(f):
        usend(f, 6, both(f, 4) + uwait(f, 2, 4) + uwait(f, 5, 4))

    def q_own(f):
        gqs[:, f * WIDE : (f + 1) * WIDE] = (
            both(f, 0) + uwait(f, 3, 0) + uwait(f, 4, 0) + uwait(f, 6, 0)
        )

    part_q(0)
    part_q(1)
    gd[...] = part_d((y + 1) % 4)
    gc[0].wait_recv()
    gd[0:MID] = gd[0:MID] + halfs[0].astype(f32)
    pd1[...] = gd[...].astype(bf16)
    begun(gc[2])
    q_far(0)
    gd[...] = part_d((y + 3) % 4)
    gc[1].wait_recv()
    gd[MID:] = gd[MID:] + halfs[1].astype(f32)
    pdm[...] = gd[...].astype(bf16)
    begun(gc[3])
    q_far(1)
    part_q(2)
    part_q(3)
    q_near(0)
    q_far(2)
    q_near(1)
    q_far(3)
    gd[...] = part_d(y)
    q_near(2)
    q_across(0)
    q_near(3)
    q_across(1)
    q_own(0)
    gc[2].wait_recv()
    gc[3].wait_recv()
    gd[...] = gd[...] + r1[...].astype(f32) + r2[...].astype(f32)
    xsend[...] = jnp.where(low == 0, gd[:, FEATS:], gd[:, :FEATS]).astype(bf16)
    begun(gc[4])
    q_across(2)
    q_own(1)
    q_across(3)
    q_own(2)

    gc[4].wait_recv()
    gd[:, 0:FEATS] = jnp.where(low == 0, gd[:, :FEATS], gd[:, FEATS:]) + xrecv[...].astype(f32)
    fd = jnp.sum(gd[:, 0:FEATS] * (xd[...].astype(f32) * gain[...]), axis=1, keepdims=True)
    e3s[...] = to_lanes(fd)
    e3 = (e3s, e3r, e3_s, e3_r, TP, t, by_tensor)
    exchange(*e3)

    q_own(3)
    eq = emb[pl.ds(pl.multiple_of(ROWS + mine * TILE, TILE), N3)].astype(f32)
    dots = jnp.sum(gqs[...] * eq, axis=1, keepdims=True)
    scale = invq[pl.ds(pl.multiple_of(mine * TILE, TILE), N3), 0:1]
    gqs[...] = (gqs[...] - eq * dots) * scale
    for f in range(4):
        asend[f] = gqs[:, f * WIDE : f * WIDE + FEATS].astype(bf16)
        asend[4 + f] = gqs[:, f * WIDE + FEATS : (f + 1) * WIDE].astype(bf16)

    def tcopy(k, n):
        to = (t + k) % TP
        return copy(
            asend.at[to, pl.ds(0, n)], arecv.at[rows_at(mine, n)], t_s.at[k], t_r.at[k], (d, to)
        )

    def trecv(k, n):
        s = (t + TP - k) % TP
        at = arecv.at[rows_at(begin(d4, s), n)]
        return copy(at, at, t_s.at[k], t_r.at[k], (d, s))

    @pl.loop(1, TP)
    def _(k):
        sized(extra, lambda n: tcopy(k, n).start())

    @sent.append
    def _():
        @pl.loop(1, TP)
        def _(k):
            sized(extra, lambda n: tcopy(k, n).wait_send())

    def tlocal(n):
        arecv[rows_at(mine, n)] = asend[t, pl.ds(0, n)]

    sized(extra, tlocal)

    finish(*e3)
    col = to_rows(total(e3r, TP)[0:1])[:, 0:1]
    iv = invd[:, 0:1]
    h = xd[...].astype(f32)
    gx = iv * gd[:, 0:FEATS] - h * gain[...] * (iv * iv * iv * col)
    outd[...] = (gx * gain[...]).astype(bf16)
    outs = [pltpu.make_async_copy(outd, od, io.at[0]), pltpu.make_async_copy(outq, oq, io.at[1])]
    outs[0].start()
    gg = jnp.sum(gx * h, axis=0, keepdims=True)

    @pl.loop(1, TP)
    def _(k):
        sized(d4 == ((t + TP - k) % TP) // 2, lambda n: trecv(k, n).wait_recv())

    gx = arecv[...].astype(f32)
    gg = gg + jnp.sum(gx * xq[...].astype(f32), axis=0, keepdims=True)
    cs4[...] = jnp.broadcast_to(gg, (8, FEATS))
    c4 = copy(cs4, cr4, c_s.at[2], c_r.at[2], sibling)
    begun(c4)
    outq[...] = (gx * gain[...]).astype(bf16)
    outs[1].start()
    c4.wait_recv()
    e4s[...] = cs4[...] + cr4[...]
    e4 = (e4s, e4r, e4_s, e4_r, 8, hz, by_hz)
    exchange(*e4)
    finish(*e4)
    ogain[...] = total(e4r, 8)[0:1]
    for c in outs:
        c.wait()

    for wait in sent:
        wait()


def shards(query_states, doc_states, gain, positives):
    vm = pl.BlockSpec(memory_space=pltpu.VMEM)
    hbm = pl.BlockSpec(memory_space=pl.ANY)
    S = pltpu.VMEM
    dma = lambda n: pltpu.SemaphoreType.DMA((n,))
    pair = lambda n: [dma(n), dma(n)]
    scratch = [
        S((ROWS, FEATS), bf16), S((ROWS, FEATS), bf16),
        S((ROWS, FEATS), bf16), S((ROWS, FEATS), bf16), S((1, FEATS), f32),
        S((2 * ROWS + TILE, FULL), bf16), S((TAKE, FULL), bf16),
        S((ROWS + TILE, 128), f32), S((ROWS, 128), f32),
        S((2 * ROWS, TAKE), f32), S((2 * ROWS, TAKE), bf16), S((TAKE, 2 * ROWS), bf16),
        S((8, ROWS), f32), S((TP, 8, ROWS), f32),
        S((8, TAKE), f32), S((8, TAKE), f32), S((8, TAKE), f32), S((8, 8, TAKE), f32),
        S((8, ROWS), f32), S((TP, 8, ROWS), f32),
        S((8, ROWS), f32), S((TP, 8, ROWS), f32),
        S((8, FEATS), f32), S((8, FEATS), f32), S((8, FEATS), f32), S((8, 8, FEATS), f32),
        S((DP, 8, 128), f32),
        S((TAKE + TILE, FULL), bf16), S((8, 3 * TILE, FULL), bf16),
        S((7, 3 * TILE, FULL), bf16), S((7, 3 * TILE, FULL), bf16),
        S((ROWS, WIDE), bf16), S((ROWS, WIDE), bf16), S((ROWS, WIDE), bf16),
        S((2, ROWS // 2, WIDE), bf16), S((ROWS, WIDE), bf16), S((ROWS, WIDE), bf16),
        S((ROWS, WIDE), f32), S((ROWS, FEATS), bf16), S((ROWS, FEATS), bf16),
        S((TP, 3 * TILE, FEATS), bf16), S((ROWS, FEATS), bf16), S((3 * TILE, FULL), f32),
        S((ROWS, FEATS), bf16), S((ROWS, FEATS), bf16),
    ]
    sems = (
        pair(1 + 2 * NCH) + pair(TP) + pair(8) + pair(TP) + pair(TP) + pair(8) + pair(8)
        + pair(8 * NCH) + pair(64) + [dma(4)] + pair(32) + pair(32) + pair(5) + pair(TP)
        + pair(3) + [dma(2)]
    )
    padded = jnp.pad(positives, (0, 3 * 128 - ROWS)).reshape(3, 128)
    parts = jnp.concatenate([padded // 128, padded % 128, jnp.zeros((2, 128), jnp.int32)])
    gq, gdoc, ggain, loss = pl.pallas_call(
        step,
        name="infonce_step",
        out_shape=(
            jax.ShapeDtypeStruct((ROWS, FEATS), bf16),
            jax.ShapeDtypeStruct((ROWS, FEATS), bf16),
            jax.ShapeDtypeStruct((1, FEATS), f32),
            jax.ShapeDtypeStruct((1, 1), f32),
        ),
        in_specs=[hbm, hbm, vm, vm],
        out_specs=(hbm, hbm, vm, vm),
        scratch_shapes=scratch + sems,
        compiler_params=pltpu.CompilerParams(
            collective_id=0, has_side_effects=True, vmem_limit_bytes=56 * 2**20
        ),
        cost_estimate=pl.CostEstimate(
            flops=7_000_000_000, bytes_accessed=3_000_000, transcendentals=1_000_000
        ),
    )(query_states, doc_states, gain[None, :], parts.astype(f32))
    return gq, gdoc, ggain[0], loss[0, 0]


def solution(mesh):
    return jax.shard_map(
        shards,
        mesh=mesh,
        in_specs=(P("dp", "tensor"), P("dp", "tensor"), P("tensor"), P("dp")),
        out_specs=(P("dp", "tensor"), P("dp", "tensor"), P("tensor"), P()),
        check_vma=False,
    )
```

time: 619 us -> 128 us (0.21)
  waiting for transfers between devices: 477 us -> 0 us
  Pallas kernels: 0 us -> 120 us
  blocking collectives: 70.1 us -> 0 us
  matrix products: 29.7 us -> 0 us
  other arithmetic: 25.3 us -> 0.68 us
  between operations: 15.7 us -> 2.43 us
    psum x1 -> x0, waiting for transfers between devices: 224 us -> none  [shards(): logit_d, logit_q = lax.psum((part_d, part_q), 'tensor')]
    reduce_scatter x1 -> x0, waiting for transfers between devices: 140 us -> none  [shards(): lax.psum_scatter(jnp.concatenate([contract_rows(weight_d, query_emb), con...]
    pallas_call x0 -> x1, Pallas kernels: none -> 120 us  [shards(): pl.pallas_call(step, name='infonce_step', out_shape=(jax.ShapeDtypeStruct...]
    all_gather x2 -> x0, waiting for transfers between devices: 113 us -> none  [the longest x1 60.7 us: shards(): lax.all_gather(query_emb, 'dp', axis=0, tiled=True)]
    psum x3 -> x0, blocking collectives: 70.1 us -> none  [the longest x1 37.9 us: shards(): grad_gain, loss_sum = lax.psum((gain_local, loss_rows), 'dp')]
    dot_general x6 -> x0, matrix products: 29.7 us -> none  [the longest x2 12.7 us: contract_cols(): lax.dot_general(left, right, (((1,), (1,)), ((), ())), preferred_element_...]
    reduce_sum x4 -> x0, other arithmetic: 8.22 us -> none  [the longest x1 5.08 us: shards(): posit = jnp.sum(jnp.where(hit, logit_d, 0.0), axis=1)]
    mul x2 -> x0, other arithmetic: 6.95 us -> none  [the longest x1 6.94 us: shards(): jnp.concatenate([contract_rows(weight_d, query_emb), contract_rows(weight...]
  transfers between devices with their start and end apart: 4 -> 0, of which waited for: 4 -> 0; matrix products, arithmetic and copies ran while one was open for 2% -> 0% of each run, Pallas kernels for 0% -> 0%
where the time goes in v2:
time: 128 us; the launch traced here: 127 us
  Pallas kernels  120 us (94%)
  local copies, waits for them, and re-layouts  3.71 us (3%)
  between operations  2.43 us (2%)
    pallas_call x1, Pallas kernels, shards(): pl.pallas_call(step, name='infonce_step', out_shape=(jax.ShapeDtypeStruct...  120 us
    unnamed x9, local copies, waits for them, and re-layouts  3.63 us

profile of v2, /device:TPU:1, one launch (start us, length us, event | category | flops | bytes accessed | tf_op | source)
XLA Modules:
  0.0 127.2 jit_solution(4147303629219918632)
XLA Ops:
  0.6 0.0 copy-start.1
  0.7 0.1 pad.7.clone
  0.7 0.6 copy-done.1
  1.3 0.7 add_convert_fusion.pos
  2.0 120.3 %infonce_step.1 = (bf16[288,448]{1,0:T(8,128)(2,1)}, bf16[288,448]{1,0:T(8,128)(2,1)}, f32[1,448]{1,0:T(1,128)}, f32[1,1]{1,0:T(1,128)}) custom-call(bf16[288,448]{1,0:T(8,128)(2,1)} %hq.1, bf16[288,448]{1,0:T(8,128)(2,1)} %hd.1, f32[1,448]{1,0:T(1,128)} %bitcast.26, f32[8,128]{1,0:T(8,128)} %add_convert_fusion.pos), custom_call_target="tpu_custom_call" | custom-call | flops 7000000000 | bytes 3000000 | tf_op jit(solution)/shard_map/infonce_step/pallas_call | solution.py:643
  122.3 0.0 copy-start
  122.4 1.7 %copy.12 = bf16[288,448]{1,0:T(8,128)(2,1)} copy(bf16[288,448]{1,0:T(8,128)(2,1)} %get-tuple-element.18) | data formatting | bytes 516096
  124.1 0.0 copy-done
  124.1 0.0 copy-start.2
  124.1 0.7 copy.13
  124.8 0.0 copy-done.2
  124.8 0.6 copy.14
  (2 shorter events, 0.0 us)
Async XLA Ops:
  0.6 0.7 copy-start.1
  122.3 1.8 %copy-start = (bf16[288,448]{1,0:T(8,128)(2,1)S(1)}, bf16[288,448]{1,0:T(8,128)(2,1)}, u32[]{:S(2)}) copy-start(bf16[288,448]{1,0:T(8,128)(2,1)} %get-tuple-element.19) | copy-start | bytes 774148
  124.1 0.7 copy-start.2

commit v3 on v2

--- a/solution.py
+++ b/solution.py
@@ -33,12 +33,12 @@
 def step(
     hq, hd, gain, pos,
     oq, od, ogain, oloss,
-    xq, xd, pq, pd, gpart, emb, qi, invq, invd, logits, wts, wtt,
-    e0s, e0r, cs1, cr1, e1s, e1r, e2s, e2r, e3s, e3r, cs4, cr4, e4s, e4r, epr,
+    xq, xd, pq, pd, gfull, raw, emb, qi, invq, invd, logits, stat, wts, wtt,
+    e0s, e0r, cr1, e1s, e1r, e2s, e2r, e3s, e3r, cs4, cr4, e4s, e4r, epr,
     partq, sibr, sendq, recvq, pd2, pd1, pdm, halfs, r1, r2, gd, xsend, xrecv,
-    asend, arecv, gqs, outq, outd,
+    asend, arecv, dsend, drecv, outq, outd,
     x_s, x_r, e0_s, e0_r, e1_s, e1_r, e2_s, e2_r, e3_s, e3_r, e4_s, e4_r, ep_s, ep_r,
-    y_s, y_r, a_s, a_r, loc, b_s, b_r, u_s, u_r, g_s, g_r, t_s, t_r, c_s, c_r, io,
+    y_s, y_r, a_s, a_r, loc, b_s, b_r, u_s, u_r, g_s, g_r, t_s, t_r, v_s, v_r, c_s, c_r, io,
 ):
     d = lax.axis_index("dp")
     t = lax.axis_index("tensor")
@@ -118,14 +118,14 @@
     nd = xd[...].astype(f32) * gain[...]
     lq = to_lanes(jnp.sum(nq * nq, axis=1, keepdims=True))
     ld = to_lanes(jnp.sum(nd * nd, axis=1, keepdims=True))
-    e0s[...] = jnp.where(sub8(ROWS) == 0, lq, ld)
+    e0s[...] = jnp.broadcast_to(gain[...], (8, FEATS))
+    e0s[0:1, 0:ROWS] = lq[0:1]
+    e0s[1:2, 0:ROWS] = ld[0:1]
     pl.semaphore_wait(barrier, TP + 7)
 
     def xcopy(i):
-        if i == 0:
-            return copy(gain, gpart, x_s.at[0], x_r.at[0], partner)
-        src, dst = (xq, pq) if i <= NCH else (xd, pd)
-        part = pl.ds(((i - 1) % NCH) * CHUNK, CHUNK)
+        src, dst = (xq, pq) if i < NCH else (xd, pd)
+        part = pl.ds((i % NCH) * CHUNK, CHUNK)
         return copy(src.at[part], dst.at[part], x_s.at[i], x_r.at[i], partner)
 
     def begun(c):
@@ -162,32 +162,34 @@
 
     e0 = (e0s, e0r, e0_s, e0_r, TP, t, by_tensor)
     begun(xcopy(0))
-    begun(xcopy(1))
     exchange(*e0)
-    for i in range(2, 1 + 2 * NCH):
+    for i in range(1, 2 * NCH):
         begun(xcopy(i))
 
     mine = begin(d4, t)
     here = place(hz, core, t)
     extra = d4 == third
 
-    finish(*e0)
-    inv = lax.rsqrt(total(e0r, TP) + eps_len)
-    invq[0:ROWS] = to_rows(inv[0:1])
-    invd[...] = to_rows(inv[1:2])
-
     def pack(a, k):
-        own, part, inverse, base = (xq, pq, invq, ROWS) if a == 0 else (xd, pd, invd, 0)
-        xcopy(1 + a * NCH + k).wait_recv()
+        own, part, base = (xq, pq, ROWS) if a == 0 else (xd, pd, 0)
+        xcopy(a * NCH + k).wait_recv()
         rs = pl.ds(k * CHUNK, CHUNK)
-        scale = inverse[rs, 0:1]
-        eo = own[rs].astype(f32) * gain[...] * scale
-        ep = part[rs].astype(f32) * gpart[...] * scale
+        eo = own[rs].astype(f32)
+        ep = part[rs].astype(f32)
         left = jnp.where(low == 0, eo, ep)
         right = jnp.where(low == 0, ep, eo)
-        emb[pl.ds(base + k * CHUNK, CHUNK), lanes(y)] = jnp.concatenate(
+        raw[pl.ds(base + k * CHUNK, CHUNK), lanes(y)] = jnp.concatenate(
             [left, right], axis=1
         ).astype(bf16)
+
+    def normalise(a, k, block):
+        inverse, base = (invq, ROWS) if a == 0 else (invd, 0)
+        for part in range(2):
+            rs = k * CHUNK + part * HALF
+            scale = inverse[pl.ds(rs, HALF), 0:1]
+            at = pl.ds(base + rs, HALF)
+            cs = lanes(block)
+            emb[at, cs] = (raw[at, cs].astype(f32) * gfull[:, cs] * scale).astype(bf16)
 
     def ycopy(a, k, kind):
         base = (ROWS if a == 0 else 0) + k * CHUNK
@@ -198,7 +200,7 @@
             at, dev, block = pl.ds(base, HALF), up, (y + 3) % 4
         else:
             at, dev, block = pl.ds(base + HALF, HALF), down, (y + 1) % 4
-        ref = emb.at[at, lanes(block)]
+        ref = raw.at[at, lanes(block)]
         return copy(ref, ref, y_s.at[i], y_r.at[i], dev)
 
     def yrecv(a, k, kind):
@@ -206,7 +208,7 @@
         i = (a * NCH + k) * 4 + kind
         at = pl.ds(base, CHUNK) if kind < 2 else pl.ds(base + (kind - 2) * HALF, HALF)
         block = ((y + 3) % 4, (y + 1) % 4, (y + 2) % 4, (y + 2) % 4)[kind]
-        ref = emb.at[at, lanes(block)]
+        ref = raw.at[at, lanes(block)]
         copy(ref, ref, y_s.at[i], y_r.at[i], up).wait_recv()
 
     def arow(i, hz_s, core_s, n):
@@ -269,11 +271,20 @@
         def _(k):
             sized(gives(k, 1 - core), lambda n: arrived(i, k, 1 - core, 8 + k, n).wait_recv())
 
-    xcopy(0).wait_recv()
     for k in range(NCH):
         pack(0, k)
         begun(ycopy(0, k, 0))
         begun(ycopy(0, k, 1))
+    finish(*e0)
+    inv = lax.rsqrt(total(e0r, TP)[:, 0:ROWS] + eps_len)
+    invq[0:ROWS] = to_rows(inv[0:1])
+    invd[...] = to_rows(inv[1:2])
+    for b in range(4):
+        gfull[:, b * WIDE : (b + 1) * WIDE] = jnp.concatenate(
+            [e0r[b, 2:3], e0r[4 + b, 2:3]], axis=1
+        )
+    for k in range(NCH):
+        normalise(0, k, y)
     astart(0)
     ep = (pos, epr, ep_s, ep_r, 8, hz, by_hz)
     exchange(*ep)
@@ -285,12 +296,16 @@
         pack(1, k)
         begun(ycopy(1, k, 0))
         begun(ycopy(1, k, 1))
+        normalise(0, k, (y + 3) % 4)
+        normalise(0, k, (y + 1) % 4)
     astart(1)
     astart(2)
     aforward(0)
     for k in range(NCH):
+        normalise(1, k, y)
         yrecv(0, k, 2)
         yrecv(0, k, 3)
+        normalise(0, k, (y + 2) % 4)
     astart(3)
     aforward(1)
     aforward(2)
@@ -299,6 +314,9 @@
         begun(ycopy(1, k, 2))
         yrecv(1, k, 1)
         begun(ycopy(1, k, 3))
+    for k in range(NCH):
+        normalise(1, k, (y + 3) % 4)
+        normalise(1, k, (y + 1) % 4)
     aforward(3)
     for i in range(4):
         afinish(i)
@@ -316,21 +334,31 @@
     epc = copy(epr.at[pl.ds(0, 8)], epr.at[pl.ds(8, 8)], c_s.at[0], c_r.at[0], sibling)
     begun(epc)
 
-    MC = 144
+    stat[0:1] = jnp.full((1, TAKE), masked, f32)
+    stat[1:8] = jnp.zeros((7, TAKE), f32)
 
     def logit_rows(r, query):
-        at = pl.ds(pl.multiple_of(r, TILE), MC)
+        at = pl.ds(pl.multiple_of(r, TILE), CHUNK)
         s = lax.dot_general(
             emb[at], qi[...], (((1,), (1,)), ((), ())), preferred_element_type=f32
         ) * inv_temp
+        row = lax.broadcasted_iota(jnp.int32, (CHUNK, TAKE), 0)
         if query:
-            j = d * ROWS + r - ROWS + lax.broadcasted_iota(jnp.int32, (MC, TAKE), 0)
-            s = jnp.where(j == row_p, masked, s)
+            s = jnp.where(d * ROWS + r - ROWS + row == row_p, masked, s)
+        else:
+            hit = jnp.where(d * ROWS + r + row == pos_p, s, 0.0)
+            stat[2:3] = stat[2:3] + jnp.sum(hit, axis=0, keepdims=True)
         logits[at] = s
-
-    @pl.loop(0, ROWS // MC)
+        old = stat[0:1]
+        new = jnp.maximum(old, jnp.max(s, axis=0, keepdims=True))
+        stat[0:1] = new
+        stat[1:2] = stat[1:2] * jnp.exp(old - new) + jnp.sum(
+            jnp.exp(s - new), axis=0, keepdims=True
+        )
+
+    @pl.loop(0, NCH)
     def _(m):
-        logit_rows(ROWS + m * MC, True)
+        logit_rows(ROWS + m * CHUNK, True)
 
     epc.wait_recv()
     local_p = (begin(q_p, t) + off_p) * TILE + lane_p % TILE
@@ -347,28 +375,22 @@
     for k in range(NCH):
         yrecv(1, k, 2)
         yrecv(1, k, 3)
-
-    @pl.loop(0, ROWS // MC)
-    def _(m):
-        logit_rows(m * MC, False)
+        normalise(1, k, (y + 2) % 4)
+        logit_rows(k * CHUNK, False)
 
     own_j = d * ROWS + lax.broadcasted_iota(jnp.int32, (ROWS, TAKE), 0)
-    top = jnp.max(logits[...], axis=0, keepdims=True)
-    tot = jnp.sum(jnp.exp(logits[...] - top), axis=0, keepdims=True)
-    posit = jnp.sum(
-        jnp.where(own_j == pos_p, logits[0:ROWS], 0.0), axis=0, keepdims=True
-    )
     sub_t = sub8(TAKE)
-    cs1[...] = jnp.where(sub_t == 0, top, jnp.where(sub_t == 1, tot, posit))
-    c1 = copy(cs1, cr1, c_s.at[1], c_r.at[1], sibling)
+    c1 = copy(stat, cr1, c_s.at[1], c_r.at[1], sibling)
     begun(c1)
     c1.wait_recv()
+    top, tot, posit = stat[0:1], stat[1:2], stat[2:3]
     top_o = cr1[0:1]
     top_c = jnp.maximum(top, top_o)
     tot = tot * jnp.exp(top - top_c) + cr1[1:2] * jnp.exp(top_o - top_c)
     e1s[...] = jnp.where(sub_t == 0, top_c, jnp.where(sub_t == 1, tot, posit + cr1[2:3]))
     e1 = (e1s, e1r, e1_s, e1_r, 8, hz, by_hz)
     exchange(*e1)
+    pick = jnp.where(own_j == row_p, 1.0, 0.0).astype(bf16)
     finish(*e1)
     all_top = e1r[0, 0:1]
     for s in range(1, 8):
@@ -381,10 +403,16 @@
     lse = all_top + jnp.log(all_tot)
     loss_part = jnp.sum(lse - all_pos, axis=1, keepdims=True)
 
-    pick = (own_j == row_p).astype(f32)
-    lse_own = lax.dot_general(
-        jnp.broadcast_to(lse, (8, TAKE)), pick, (((1,), (1,)), ((), ())),
-        precision=HIGH, preferred_element_type=f32,
+    lse1 = lse.astype(bf16).astype(f32)
+    lse2 = (lse - lse1).astype(bf16).astype(f32)
+    split = jnp.where(
+        sub_t == 0, lse1, jnp.where(sub_t == 1, lse2, jnp.where(sub_t == 2, lse - lse1 - lse2, 0.0))
+    )
+    lse_own = jnp.sum(
+        lax.dot_general(
+            split.astype(bf16), pick, (((1,), (1,)), ((), ())), preferred_element_type=f32
+        ),
+        axis=0, keepdims=True,
     )
     e2s[...] = jnp.where(sub8(ROWS) == 0, lse_own, loss_part)
     e2 = (e2s, e2r, e2_s, e2_r, TP, t, by_tensor)
@@ -422,10 +450,13 @@
     def target(s):
         return (xh + s // 4) % 2 * 4 + (zc + s % 4) % 4
 
+    def cols(f):
+        return lanes((y + 1 + f) % 4)
+
     def bcopy(f, k, n):
         at = rows_at(place(k, 1 - core, t), n)
         return copy(
-            partq.at[at, pl.ds(f * WIDE, WIDE)], sibr.at[k, pl.ds(0, n), pl.ds(f * WIDE, WIDE)],
+            partq.at[at, cols(f)], sibr.at[k, pl.ds(0, n), cols(f)],
             b_s.at[f * 8 + k], b_r.at[f * 8 + k], sibling,
         )
 
@@ -433,9 +464,9 @@
         return (k // 4) * 2 + core_s == third
 
     def part_q(f):
-        partq[0:TAKE, f * WIDE : (f + 1) * WIDE] = (
+        partq[0:TAKE, cols(f)] = (
             jnp.dot(
-                wtt[...], emb[0 : 2 * ROWS, f * WIDE : (f + 1) * WIDE],
+                wtt[...], emb[0 : 2 * ROWS, cols(f)],
                 preferred_element_type=f32,
             ) * inv_temp
         ).astype(bf16)
@@ -455,27 +486,27 @@
     def both(f, s):
         k = target(s)
         sized(three(k, core), lambda n: bcopy(f, k, n).wait_recv())
-        cs = slice(f * WIDE, (f + 1) * WIDE)
+        cs = cols(f)
         return partq[rows_at(place(k, core, t), N3), cs].astype(f32) + sibr[k, :, cs].astype(f32)
 
     FLOW = ((2, zup), (6, zdown), (5, zup), (3, zdown), (1, zup), (7, zdown), (4, across))
 
     def ucopy(f, i, n):
-        cs = pl.ds(f * WIDE, WIDE)
+        cs = cols(f)
         return copy(
             sendq.at[i, pl.ds(0, n), cs], recvq.at[i, pl.ds(0, n), cs],
             u_s.at[f * 8 + i], u_r.at[f * 8 + i], FLOW[i][1],
         )
 
     def usend(f, i, value):
-        sendq[i, :, f * WIDE : (f + 1) * WIDE] = value.astype(bf16)
+        sendq[i, :, cols(f)] = value.astype(bf16)
         far = three(target(FLOW[i][0]), core)
         sized(far, lambda n: ucopy(f, i, n).start())
         sent.append(lambda: sized(far, lambda n: ucopy(f, i, n).wait_send()))
 
     def uwait(f, i, s):
         sized(three(target(s), core), lambda n: ucopy(f, i, n).wait_recv())
-        return recvq[i, :, f * WIDE : (f + 1) * WIDE].astype(f32)
+        return recvq[i, :, cols(f)].astype(f32)
 
     def q_far(f):
         usend(f, 0, both(f, 2))
@@ -490,10 +521,34 @@
     def q_across(f):
         usend(f, 6, both(f, 4) + uwait(f, 2, 4) + uwait(f, 5, 4))
 
+    def tcopy(f, far, n):
+        to = (y + 1 + f) % 4 + 4 * ((low + far) % 2)
+        return copy(
+            asend.at[to, pl.ds(0, n)], arecv.at[rows_at(mine, n)],
+            t_s.at[f * 2 + far], t_r.at[f * 2 + far], (d, to),
+        )
+
+    def trecv(f, far):
+        s = (y + 3 - f) % 4 + 4 * ((low + far) % 2)
+        at = lambda n: arecv.at[rows_at(begin(d4, s), n)]
+        sized(
+            d4 == s // 2,
+            lambda n: copy(at(n), at(n), t_s.at[0], t_r.at[f * 2 + far], (d, s)).wait_recv(),
+        )
+
     def q_own(f):
-        gqs[:, f * WIDE : (f + 1) * WIDE] = (
-            both(f, 0) + uwait(f, 3, 0) + uwait(f, 4, 0) + uwait(f, 6, 0)
-        )
+        g = both(f, 0) + uwait(f, 3, 0) + uwait(f, 4, 0) + uwait(f, 6, 0)
+        fb = (y + 1 + f) % 4
+        asend[fb] = g[:, :FEATS].astype(bf16)
+        asend[4 + fb] = g[:, FEATS:].astype(bf16)
+        for far in range(2):
+            if f < 3 or far == 1:
+                sized(extra, lambda n: tcopy(f, far, n).start())
+                sent.append(
+                    lambda far=far: sized(extra, lambda n: tcopy(f, far, n).wait_send())
+                )
+        eq = emb[pl.ds(pl.multiple_of(ROWS + mine * TILE, TILE), N3), lanes(fb)].astype(f32)
+        return jnp.sum(g * eq, axis=1, keepdims=True)
 
     part_q(0)
     part_q(1)
@@ -520,16 +575,16 @@
     q_across(0)
     q_near(3)
     q_across(1)
-    q_own(0)
+    dots = q_own(0)
     gc[2].wait_recv()
     gc[3].wait_recv()
     gd[...] = gd[...] + r1[...].astype(f32) + r2[...].astype(f32)
     xsend[...] = jnp.where(low == 0, gd[:, FEATS:], gd[:, :FEATS]).astype(bf16)
     begun(gc[4])
     q_across(2)
-    q_own(1)
+    dots = dots + q_own(1)
     q_across(3)
-    q_own(2)
+    dots = dots + q_own(2)
 
     gc[4].wait_recv()
     gd[:, 0:FEATS] = jnp.where(low == 0, gd[:, :FEATS], gd[:, FEATS:]) + xrecv[...].astype(f32)
@@ -538,38 +593,33 @@
     e3 = (e3s, e3r, e3_s, e3_r, TP, t, by_tensor)
     exchange(*e3)
 
-    q_own(3)
-    eq = emb[pl.ds(pl.multiple_of(ROWS + mine * TILE, TILE), N3)].astype(f32)
-    dots = jnp.sum(gqs[...] * eq, axis=1, keepdims=True)
-    scale = invq[pl.ds(pl.multiple_of(mine * TILE, TILE), N3), 0:1]
-    gqs[...] = (gqs[...] - eq * dots) * scale
-    for f in range(4):
-        asend[f] = gqs[:, f * WIDE : f * WIDE + FEATS].astype(bf16)
-        asend[4 + f] = gqs[:, f * WIDE + FEATS : (f + 1) * WIDE].astype(bf16)
-
-    def tcopy(k, n):
+    dots = dots + q_own(3)
+    dsend[...] = jnp.broadcast_to(dots, (N3, 128))
+
+    def vcopy(k, n):
         to = (t + k) % TP
         return copy(
-            asend.at[to, pl.ds(0, n)], arecv.at[rows_at(mine, n)], t_s.at[k], t_r.at[k], (d, to)
-        )
-
-    def trecv(k, n):
+            dsend.at[pl.ds(0, n)], drecv.at[rows_at(mine, n)], v_s.at[k], v_r.at[k], (d, to)
+        )
+
+    def vrecv(k, n):
         s = (t + TP - k) % TP
-        at = arecv.at[rows_at(begin(d4, s), n)]
-        return copy(at, at, t_s.at[k], t_r.at[k], (d, s))
+        at = drecv.at[rows_at(begin(d4, s), n)]
+        return copy(at, at, v_s.at[k], v_r.at[k], (d, s))
 
     @pl.loop(1, TP)
     def _(k):
-        sized(extra, lambda n: tcopy(k, n).start())
+        sized(extra, lambda n: vcopy(k, n).start())
 
     @sent.append
     def _():
         @pl.loop(1, TP)
         def _(k):
-            sized(extra, lambda n: tcopy(k, n).wait_send())
+            sized(extra, lambda n: vcopy(k, n).wait_send())
 
     def tlocal(n):
         arecv[rows_at(mine, n)] = asend[t, pl.ds(0, n)]
+        drecv[rows_at(mine, n)] = dsend[pl.ds(0, n)]
 
     sized(extra, tlocal)
 
@@ -583,12 +633,19 @@
     outs[0].start()
     gg = jnp.sum(gx * h, axis=0, keepdims=True)
 
+    for f in range(4):
+        for far in range(2):
+            if f < 3 or far == 1:
+                trecv(f, far)
+
     @pl.loop(1, TP)
     def _(k):
-        sized(d4 == ((t + TP - k) % TP) // 2, lambda n: trecv(k, n).wait_recv())
-
-    gx = arecv[...].astype(f32)
-    gg = gg + jnp.sum(gx * xq[...].astype(f32), axis=0, keepdims=True)
+        sized(d4 == ((t + TP - k) % TP) // 2, lambda n: vrecv(k, n).wait_recv())
+
+    h = xq[...].astype(f32)
+    iv = invq[0:ROWS, 0:1]
+    gx = iv * arecv[...].astype(f32) - h * gain[...] * (iv * iv * drecv[:, 0:1])
+    gg = gg + jnp.sum(gx * h, axis=0, keepdims=True)
     cs4[...] = jnp.broadcast_to(gg, (8, FEATS))
     c4 = copy(cs4, cr4, c_s.at[2], c_r.at[2], sibling)
     begun(c4)
@@ -615,12 +672,12 @@
     pair = lambda n: [dma(n), dma(n)]
     scratch = [
         S((ROWS, FEATS), bf16), S((ROWS, FEATS), bf16),
-        S((ROWS, FEATS), bf16), S((ROWS, FEATS), bf16), S((1, FEATS), f32),
-        S((2 * ROWS + TILE, FULL), bf16), S((TAKE, FULL), bf16),
+        S((ROWS, FEATS), bf16), S((ROWS, FEATS), bf16), S((1, FULL), f32),
+        S((2 * ROWS, FULL), bf16), S((2 * ROWS + TILE, FULL), bf16), S((TAKE, FULL), bf16),
         S((ROWS + TILE, 128), f32), S((ROWS, 128), f32),
-        S((2 * ROWS, TAKE), f32), S((2 * ROWS, TAKE), bf16), S((TAKE, 2 * ROWS), bf16),
-        S((8, ROWS), f32), S((TP, 8, ROWS), f32),
-        S((8, TAKE), f32), S((8, TAKE), f32), S((8, TAKE), f32), S((8, 8, TAKE), f32),
+        S((2 * ROWS, TAKE), f32), S((8, TAKE), f32), S((2 * ROWS, TAKE), bf16), S((TAKE, 2 * ROWS), bf16),
+        S((8, FEATS), f32), S((TP, 8, FEATS), f32),
+        S((8, TAKE), f32), S((8, TAKE), f32), S((8, 8, TAKE), f32),
         S((8, ROWS), f32), S((TP, 8, ROWS), f32),
         S((8, ROWS), f32), S((TP, 8, ROWS), f32),
         S((8, FEATS), f32), S((8, FEATS), f32), S((8, FEATS), f32), S((8, 8, FEATS), f32),
@@ -630,12 +687,12 @@
         S((ROWS, WIDE), bf16), S((ROWS, WIDE), bf16), S((ROWS, WIDE), bf16),
         S((2, ROWS // 2, WIDE), bf16), S((ROWS, WIDE), bf16), S((ROWS, WIDE), bf16),
         S((ROWS, WIDE), f32), S((ROWS, FEATS), bf16), S((ROWS, FEATS), bf16),
-        S((TP, 3 * TILE, FEATS), bf16), S((ROWS, FEATS), bf16), S((3 * TILE, FULL), f32),
+        S((TP, 3 * TILE, FEATS), bf16), S((ROWS, FEATS), bf16), S((3 * TILE, 128), f32), S((ROWS, 128), f32),
         S((ROWS, FEATS), bf16), S((ROWS, FEATS), bf16),
     ]
     sems = (
-        pair(1 + 2 * NCH) + pair(TP) + pair(8) + pair(TP) + pair(TP) + pair(8) + pair(8)
-        + pair(8 * NCH) + pair(64) + [dma(4)] + pair(32) + pair(32) + pair(5) + pair(TP)
+        pair(2 * NCH) + pair(TP) + pair(8) + pair(TP) + pair(TP) + pair(8) + pair(8)
+        + pair(8 * NCH) + pair(64) + [dma(4)] + pair(32) + pair(32) + pair(5) + pair(TP) + pair(TP)
         + pair(3) + [dma(2)]
     )
     padded = jnp.pad(positives, (0, 3 * 128 - ROWS)).reshape(3, 128)

time: 128 us -> 131 us (1.023)
  Pallas kernels: 120 us -> 124 us
    pallas_call x1, Pallas kernels: 120 us -> 124 us  [shards(): pl.pallas_call(step, name='infonce_step', out_shape=(jax.ShapeDtypeStruct...]
where the time goes in v3:
time: 131 us
  Pallas kernels  124 us (95%)
  local copies, waits for them, and re-layouts  3.71 us (3%)
  between operations  2.43 us (2%)
    pallas_call x1, Pallas kernels, shards(): pl.pallas_call(step, name='infonce_step', out_shape=(jax.ShapeDtypeStruct...  124 us
    unnamed x9, local copies, waits for them, and re-layouts  3.63 us

profile of v3, /device:TPU:1, one launch (start us, length us, event | category | flops | bytes accessed | tf_op | source)
XLA Modules:
  0.0 131.2 jit_solution(1746456527951350424)
XLA Ops:
  0.6 0.0 copy-start.1
  0.7 0.1 pad.7.clone
  0.7 0.6 copy-done.1
  1.3 0.7 add_convert_fusion.pos
  2.0 124.4 %infonce_step.1 = (bf16[288,448]{1,0:T(8,128)(2,1)}, bf16[288,448]{1,0:T(8,128)(2,1)}, f32[1,448]{1,0:T(1,128)}, f32[1,1]{1,0:T(1,128)}) custom-call(bf16[288,448]{1,0:T(8,128)(2,1)} %hq.1, bf16[288,448]{1,0:T(8,128)(2,1)} %hd.1, f32[1,448]{1,0:T(1,128)} %bitcast.26, f32[8,128]{1,0:T(8,128)} %add_convert_fusion.pos), custom_call_target="tpu_custom_call" | custom-call | flops 7000000000 | bytes 3000000 | tf_op jit(solution)/shard_map/infonce_step/pallas_call | solution.py:700
  126.4 0.0 copy-start
  126.4 1.7 %copy.12 = bf16[288,448]{1,0:T(8,128)(2,1)} copy(bf16[288,448]{1,0:T(8,128)(2,1)} %get-tuple-element.18) | data formatting | bytes 516096
  128.1 0.0 copy-done
  128.1 0.0 copy-start.2
  128.1 0.7 copy.13
  128.8 0.0 copy-done.2
  128.8 0.6 copy.14
  (2 shorter events, 0.0 us)
Async XLA Ops:
  0.6 0.7 copy-start.1
  126.4 1.8 %copy-start = (bf16[288,448]{1,0:T(8,128)(2,1)S(1)}, bf16[288,448]{1,0:T(8,128)(2,1)}, u32[]{:S(2)}) copy-start(bf16[288,448]{1,0:T(8,128)(2,1)} %get-tuple-element.19) | copy-start | bytes 774148
  128.1 0.7 copy-start.2

commit v4 on v3

--- a/solution.py
+++ b/solution.py
@@ -35,7 +35,7 @@
     oq, od, ogain, oloss,
     xq, xd, pq, pd, gfull, raw, emb, qi, invq, invd, logits, stat, wts, wtt,
     e0s, e0r, cr1, e1s, e1r, e2s, e2r, e3s, e3r, cs4, cr4, e4s, e4r, epr,
-    partq, sibr, sendq, recvq, pd2, pd1, pdm, halfs, r1, r2, gd, xsend, xrecv,
+    partq, sibr, sendq, recvq, acc1, acc2, pd2, pd1, pdm, halfs, r1, r2, gd, xsend, xrecv,
     asend, arecv, dsend, drecv, outq, outd,
     x_s, x_r, e0_s, e0_r, e1_s, e1_r, e2_s, e2_r, e3_s, e3_r, e4_s, e4_r, ep_s, ep_r,
     y_s, y_r, a_s, a_r, loc, b_s, b_r, u_s, u_r, g_s, g_r, t_s, t_r, v_s, v_r, c_s, c_r, io,
@@ -211,65 +211,81 @@
         ref = raw.at[at, lanes(block)]
         copy(ref, ref, y_s.at[i], y_r.at[i], up).wait_recv()
 
-    def arow(i, hz_s, core_s, n):
+    def source(s):
+        return (xh + s // 4) % 2 * 4 + (zc + 4 - s % 4) % 4
+
+    def gives(s, core_s):
+        return (xh + s // 4) % 2 * 2 + core_s == third
+
+    def device(s):
+        return ((xh + s // 4) % 2 * 8 + (zc + s % 4) % 4 * 2 + core, t)
+
+    def spot(i, s, core_s, n):
         block = (y + (0, 3, 1, 2)[i]) % 4
-        return qi.at[rows_at(place(hz_s, core_s, t), n), lanes(block)]
+        return qi.at[rows_at(place(source(s), core_s, t), n), lanes(block)]
 
     def own_rows(i, n):
         block = (y + (0, 3, 1, 2)[i]) % 4
         return emb.at[pl.ds(pl.multiple_of(ROWS + mine * TILE, TILE), n), lanes(block)]
 
-    def acopy(i, k, n):
-        to = (hz + k) % 8 * 2 + jnp.where(k == 0, 1 - core, core)
-        return copy(
-            own_rows(i, n), arow(i, hz, core, n), a_s.at[i * 16 + k], a_r.at[i * 16 + k], (to, t)
-        )
+    def give_own(i, slot, dev):
+        def c(n):
+            return copy(
+                own_rows(i, n), spot(i, 0, core, n), a_s.at[i * 16 + slot], a_r.at[i * 16 + slot], dev
+            )
+
+        sized(extra, lambda n: c(n).start())
+        sent.append(lambda: sized(extra, lambda n: c(n).wait_send()))
+
+    def pass_on(i, s, slot, dev):
+        def c(n):
+            ref = spot(i, s, core, n)
+            return copy(ref, ref, a_s.at[i * 16 + slot], a_r.at[i * 16 + slot], dev)
+
+        sized(gives(s, core), lambda n: c(n).start())
+        sent.append(lambda: sized(gives(s, core), lambda n: c(n).wait_send()))
+
+    def agot(i, s):
+        def c(n):
+            ref = spot(i, s, core, n)
+            copy(ref, ref, a_s.at[i * 16 + s], a_r.at[i * 16 + s], sibling).wait_recv()
+
+        sized(gives(s, core), c)
 
     def alocal(i, n):
-        return pltpu.make_async_copy(own_rows(i, n), arow(i, hz, core, n), loc.at[i])
-
-    def arrived(i, k, core_s, slot, n):
-        ref = arow(i, (hz + 8 - k) % 8, core_s, n)
-        return copy(ref, ref, a_s.at[i * 16 + slot], a_r.at[i * 16 + slot], sibling)
-
-    def gives(k, core_s):
-        return (((hz + 8 - k) % 8) // 4) * 2 + core_s == third
+        return pltpu.make_async_copy(own_rows(i, n), spot(i, 0, core, n), loc.at[i])
 
     def astart(i):
-        @pl.loop(0, 8)
-        def _(k):
-            sized(extra, lambda n: acopy(i, k, n).start())
-
+        for s in (1, 3, 2, 4) if i < 3 else (4, 1, 3, 2, 5, 7, 6):
+            give_own(i, s, device(s))
+        give_own(i, 8, sibling)
         sized(extra, lambda n: alocal(i, n).start())
 
-        @sent.append
-        def _():
-            @pl.loop(0, 8)
-            def _(k):
-                sized(extra, lambda n: acopy(i, k, n).wait_send())
-
-    def aforward(i):
-        @pl.loop(1, 8)
-        def _(k):
-            def pass_on(n):
-                arrived(i, k, core, k, n).wait_recv()
-                arrived(i, k, core, 8 + k, n).start()
-
-            sized(gives(k, core), pass_on)
-
-        @sent.append
-        def _():
-            @pl.loop(1, 8)
-            def _(k):
-                sized(gives(k, core), lambda n: arrived(i, k, core, 8 + k, n).wait_send())
+    def amid(i):
+        agot(i, 4)
+        if i < 3:
+            for s in (1, 3, 2):
+                pass_on(i, 4, 4 + s, device(s))
+        pass_on(i, 4, 12, sibling)
+        for s in (1, 3, 2):
+            agot(i, s)
+            pass_on(i, s, 8 + s, sibling)
+
+    def alast(i):
+        for s in (5, 7, 6):
+            agot(i, s)
+            pass_on(i, s, 8 + s, sibling)
 
     def afinish(i):
         sized(extra, lambda n: alocal(i, n).wait())
-        sized(gives(0, 1 - core), lambda n: arrived(i, 0, 1 - core, 0, n).wait_recv())
-
-        @pl.loop(1, 8)
-        def _(k):
-            sized(gives(k, 1 - core), lambda n: arrived(i, k, 1 - core, 8 + k, n).wait_recv())
+
+        @pl.loop(0, 8)
+        def _(s):
+            def c(n):
+                ref = spot(i, s, 1 - core, n)
+                copy(ref, ref, a_s.at[i * 16], a_r.at[i * 16 + 8 + s], sibling).wait_recv()
+
+            sized(gives(s, 1 - core), c)
 
     for k in range(NCH):
         pack(0, k)
@@ -300,24 +316,28 @@
         normalise(0, k, (y + 1) % 4)
     astart(1)
     astart(2)
-    aforward(0)
+    amid(0)
     for k in range(NCH):
         normalise(1, k, y)
         yrecv(0, k, 2)
         yrecv(0, k, 3)
         normalise(0, k, (y + 2) % 4)
     astart(3)
-    aforward(1)
-    aforward(2)
+    alast(0)
+    amid(1)
+    amid(2)
     for k in range(NCH):
         yrecv(1, k, 0)
         begun(ycopy(1, k, 2))
         yrecv(1, k, 1)
         begun(ycopy(1, k, 3))
+    alast(1)
+    alast(2)
     for k in range(NCH):
         normalise(1, k, (y + 3) % 4)
         normalise(1, k, (y + 1) % 4)
-    aforward(3)
+    amid(3)
+    alast(3)
     for i in range(4):
         afinish(i)
 
@@ -337,18 +357,12 @@
     stat[0:1] = jnp.full((1, TAKE), masked, f32)
     stat[1:8] = jnp.zeros((7, TAKE), f32)
 
-    def logit_rows(r, query):
-        at = pl.ds(pl.multiple_of(r, TILE), CHUNK)
-        s = lax.dot_general(
-            emb[at], qi[...], (((1,), (1,)), ((), ())), preferred_element_type=f32
-        ) * inv_temp
-        row = lax.broadcasted_iota(jnp.int32, (CHUNK, TAKE), 0)
-        if query:
-            s = jnp.where(d * ROWS + r - ROWS + row == row_p, masked, s)
-        else:
-            hit = jnp.where(d * ROWS + r + row == pos_p, s, 0.0)
-            stat[2:3] = stat[2:3] + jnp.sum(hit, axis=0, keepdims=True)
-        logits[at] = s
+    def product(rows, cs):
+        return lax.dot_general(
+            emb[rows, cs], qi[:, cs], (((1,), (1,)), ((), ())), preferred_element_type=f32
+        )
+
+    def statistics(s):
         old = stat[0:1]
         new = jnp.maximum(old, jnp.max(s, axis=0, keepdims=True))
         stat[0:1] = new
@@ -356,9 +370,13 @@
             jnp.exp(s - new), axis=0, keepdims=True
         )
 
-    @pl.loop(0, NCH)
-    def _(m):
-        logit_rows(ROWS + m * CHUNK, True)
+    own_j = d * ROWS + lax.broadcasted_iota(jnp.int32, (ROWS, TAKE), 0)
+    logits[ROWS:] = product(pl.ds(ROWS, ROWS), slice(None))
+    logits[ROWS:] = jnp.where(own_j == row_p, masked, logits[ROWS:] * inv_temp)
+    statistics(logits[ROWS:])
+    logits[0:ROWS] = product(pl.ds(0, ROWS), lanes(y))
+    for b in (1, 3):
+        logits[0:ROWS] = logits[0:ROWS] + product(pl.ds(0, ROWS), lanes((y + b) % 4))
 
     epc.wait_recv()
     local_p = (begin(q_p, t) + off_p) * TILE + lane_p % TILE
@@ -376,9 +394,10 @@
         yrecv(1, k, 2)
         yrecv(1, k, 3)
         normalise(1, k, (y + 2) % 4)
-        logit_rows(k * CHUNK, False)
-
-    own_j = d * ROWS + lax.broadcasted_iota(jnp.int32, (ROWS, TAKE), 0)
+    logits[0:ROWS] = (logits[0:ROWS] + product(pl.ds(0, ROWS), lanes((y + 2) % 4))) * inv_temp
+    stat[2:3] = jnp.sum(jnp.where(own_j == pos_p, logits[0:ROWS], 0.0), axis=0, keepdims=True)
+    statistics(logits[0:ROWS])
+
     sub_t = sub8(TAKE)
     c1 = copy(stat, cr1, c_s.at[1], c_r.at[1], sibling)
     begun(c1)
@@ -427,16 +446,28 @@
         ) * inv_temp
 
     MID = ROWS // 2
+    front, rear = pl.ds(0, MID), pl.ds(MID, MID)
+    gc = [
+        copy(pd2.at[front], halfs.at[0], g_s.at[0], g_r.at[0], up),
+        copy(pd2.at[rear], halfs.at[1], g_s.at[1], g_r.at[1], down),
+        copy(pd1.at[rear], r1.at[rear], g_s.at[2], g_r.at[2], up),
+        copy(pdm.at[front], r2.at[front], g_s.at[3], g_r.at[3], down),
+        copy(pd1.at[front], r1.at[front], g_s.at[4], g_r.at[4], up),
+        copy(pdm.at[rear], r2.at[rear], g_s.at[5], g_r.at[5], down),
+        copy(xsend, xrecv, g_s.at[6], g_r.at[6], partner),
+    ]
     pd2[...] = part_d((y + 2) % 4).astype(bf16)
-    gc = [
-        copy(pd2.at[pl.ds(0, MID)], halfs.at[0], g_s.at[0], g_r.at[0], up),
-        copy(pd2.at[pl.ds(MID, MID)], halfs.at[1], g_s.at[1], g_r.at[1], down),
-        copy(pd1, r1, g_s.at[2], g_r.at[2], up),
-        copy(pdm, r2, g_s.at[3], g_r.at[3], down),
-        copy(xsend, xrecv, g_s.at[4], g_r.at[4], partner),
-    ]
     begun(gc[0])
     begun(gc[1])
+    gd[...] = part_d((y + 1) % 4)
+    pd1[rear] = gd[rear].astype(bf16)
+    begun(gc[2])
+    acc1[...] = gd[front]
+    gd[...] = part_d((y + 3) % 4)
+    pdm[front] = gd[front].astype(bf16)
+    begun(gc[3])
+    acc2[...] = gd[rear]
+    gd[...] = part_d(y)
 
     finish(*e2)
     sums = total(e2r, TP)
@@ -536,8 +567,30 @@
             lambda n: copy(at(n), at(n), t_s.at[0], t_r.at[f * 2 + far], (d, s)).wait_recv(),
         )
 
+    def direct(f, s, n):
+        cs = cols(f)
+        return copy(
+            sendq.at[s - 1, pl.ds(0, n), cs], recvq.at[s - 1, pl.ds(0, n), cs],
+            u_s.at[f * 8 + s - 1], u_r.at[f * 8 + s - 1], device(s),
+        )
+
+    def q_direct(f):
+        for s in (5, 7, 6, 4, 2, 1, 3):
+            sendq[s - 1, :, cols(f)] = both(f, s).astype(bf16)
+            far = three(target(s), core)
+            sized(far, lambda n: direct(f, s, n).start())
+            sent.append(
+                lambda s=s, far=far: sized(far, lambda n: direct(f, s, n).wait_send())
+            )
+
     def q_own(f):
-        g = both(f, 0) + uwait(f, 3, 0) + uwait(f, 4, 0) + uwait(f, 6, 0)
+        if f < 3:
+            g = both(f, 0) + uwait(f, 3, 0) + uwait(f, 4, 0) + uwait(f, 6, 0)
+        else:
+            g = both(f, 0)
+            for s in range(1, 8):
+                sized(extra, lambda n: direct(f, s, n).wait_recv())
+                g = g + recvq[s - 1, :, cols(f)].astype(f32)
         fb = (y + 1 + f) % 4
         asend[fb] = g[:, :FEATS].astype(bf16)
         asend[4 + fb] = g[:, FEATS:].astype(bf16)
@@ -551,47 +604,40 @@
         return jnp.sum(g * eq, axis=1, keepdims=True)
 
     part_q(0)
+    gc[0].wait_recv()
+    pd1[front] = (acc1[...] + halfs[0].astype(f32)).astype(bf16)
+    begun(gc[4])
+    gc[1].wait_recv()
+    pdm[rear] = (acc2[...] + halfs[1].astype(f32)).astype(bf16)
+    begun(gc[5])
     part_q(1)
-    gd[...] = part_d((y + 1) % 4)
-    gc[0].wait_recv()
-    gd[0:MID] = gd[0:MID] + halfs[0].astype(f32)
-    pd1[...] = gd[...].astype(bf16)
-    begun(gc[2])
     q_far(0)
-    gd[...] = part_d((y + 3) % 4)
-    gc[1].wait_recv()
-    gd[MID:] = gd[MID:] + halfs[1].astype(f32)
-    pdm[...] = gd[...].astype(bf16)
-    begun(gc[3])
+    part_q(2)
     q_far(1)
-    part_q(2)
     part_q(3)
     q_near(0)
     q_far(2)
     q_near(1)
-    q_far(3)
-    gd[...] = part_d(y)
+    q_direct(3)
+    q_across(0)
     q_near(2)
-    q_across(0)
-    q_near(3)
+    for i in range(2, 6):
+        gc[i].wait_recv()
+    gd[...] = gd[...] + r1[...].astype(f32) + r2[...].astype(f32)
+    xsend[...] = jnp.where(low == 0, gd[:, FEATS:], gd[:, :FEATS]).astype(bf16)
+    begun(gc[6])
     q_across(1)
     dots = q_own(0)
-    gc[2].wait_recv()
-    gc[3].wait_recv()
-    gd[...] = gd[...] + r1[...].astype(f32) + r2[...].astype(f32)
-    xsend[...] = jnp.where(low == 0, gd[:, FEATS:], gd[:, :FEATS]).astype(bf16)
-    begun(gc[4])
     q_across(2)
     dots = dots + q_own(1)
-    q_across(3)
-    dots = dots + q_own(2)
-
-    gc[4].wait_recv()
+
+    gc[6].wait_recv()
     gd[:, 0:FEATS] = jnp.where(low == 0, gd[:, :FEATS], gd[:, FEATS:]) + xrecv[...].astype(f32)
     fd = jnp.sum(gd[:, 0:FEATS] * (xd[...].astype(f32) * gain[...]), axis=1, keepdims=True)
     e3s[...] = to_lanes(fd)
     e3 = (e3s, e3r, e3_s, e3_r, TP, t, by_tensor)
     exchange(*e3)
+    dots = dots + q_own(2)
 
     dots = dots + q_own(3)
     dsend[...] = jnp.broadcast_to(dots, (N3, 128))
@@ -684,6 +730,7 @@
         S((DP, 8, 128), f32),
         S((TAKE + TILE, FULL), bf16), S((8, 3 * TILE, FULL), bf16),
         S((7, 3 * TILE, FULL), bf16), S((7, 3 * TILE, FULL), bf16),
+        S((ROWS // 2, WIDE), f32), S((ROWS // 2, WIDE), f32),
         S((ROWS, WIDE), bf16), S((ROWS, WIDE), bf16), S((ROWS, WIDE), bf16),
         S((2, ROWS // 2, WIDE), bf16), S((ROWS, WIDE), bf16), S((ROWS, WIDE), bf16),
         S((ROWS, WIDE), f32), S((ROWS, FEATS), bf16), S((ROWS, FEATS), bf16),
@@ -692,7 +739,7 @@
     ]
     sems = (
         pair(2 * NCH) + pair(TP) + pair(8) + pair(TP) + pair(TP) + pair(8) + pair(8)
-        + pair(8 * NCH) + pair(64) + [dma(4)] + pair(32) + pair(32) + pair(5) + pair(TP) + pair(TP)
+        + pair(8 * NCH) + pair(64) + [dma(4)] + pair(32) + pair(32) + pair(7) + pair(TP) + pair(TP)
         + pair(3) + [dma(2)]
     )
     padded = jnp.pad(positives, (0, 3 * 128 - ROWS)).reshape(3, 128)

time: 131 us -> 127 us (0.969)
  Pallas kernels: 124 us -> 120 us
    pallas_call x1, Pallas kernels: 124 us -> 120 us  [shards(): pl.pallas_call(step, name='infonce_step', out_shape=(jax.ShapeDtypeStruct...]
where the time goes in v4:
time: 127 us; the launch traced here: 126 us
  Pallas kernels  120 us (94%)
  local copies, waits for them, and re-layouts  3.71 us (3%)
  between operations  2.43 us (2%)
    pallas_call x1, Pallas kernels, shards(): pl.pallas_call(step, name='infonce_step', out_shape=(jax.ShapeDtypeStruct...  120 us
    unnamed x9, local copies, waits for them, and re-layouts  3.63 us

profile of v4, /device:TPU:1, one launch (start us, length us, event | category | flops | bytes accessed | tf_op | source)
XLA Modules:
  0.0 126.4 jit_solution(10790843878957815340)
XLA Ops:
  0.6 0.0 copy-start.1
  0.7 0.1 pad.7.clone
  0.7 0.6 copy-done.1
  1.3 0.7 add_convert_fusion.pos
  2.0 119.6 %infonce_step.1 = (bf16[288,448]{1,0:T(8,128)(2,1)}, bf16[288,448]{1,0:T(8,128)(2,1)}, f32[1,448]{1,0:T(1,128)}, f32[1,1]{1,0:T(1,128)}) custom-call(bf16[288,448]{1,0:T(8,128)(2,1)} %hq.1, bf16[288,448]{1,0:T(8,128)(2,1)} %hd.1, f32[1,448]{1,0:T(1,128)} %bitcast.26, f32[8,128]{1,0:T(8,128)} %add_convert_fusion.pos), custom_call_target="tpu_custom_call" | custom-call | flops 7000000000 | bytes 3000000 | tf_op jit(solution)/shard_map/infonce_step/pallas_call | solution.py:747
  121.6 0.0 copy-start
  121.6 1.7 %copy.12 = bf16[288,448]{1,0:T(8,128)(2,1)} copy(bf16[288,448]{1,0:T(8,128)(2,1)} %get-tuple-element.18) | data formatting | bytes 516096
  123.3 0.0 copy-done
  123.4 0.0 copy-start.2
  123.4 0.7 copy.13
  124.1 0.0 copy-done.2
  124.1 0.6 copy.14
  (2 shorter events, 0.0 us)
Async XLA Ops:
  0.6 0.7 copy-start.1
  121.6 1.8 %copy-start = (bf16[288,448]{1,0:T(8,128)(2,1)S(1)}, bf16[288,448]{1,0:T(8,128)(2,1)}, u32[]{:S(2)}) copy-start(bf16[288,448]{1,0:T(8,128)(2,1)} %get-tuple-element.19) | copy-start | bytes 774148
  123.4 0.7 copy-start.2

commit v5 on v4

--- a/solution.py
+++ b/solution.py
@@ -34,7 +34,7 @@
     hq, hd, gain, pos,
     oq, od, ogain, oloss,
     xq, xd, pq, pd, gfull, raw, emb, qi, invq, invd, logits, stat, wts, wtt,
-    e0s, e0r, cr1, e1s, e1r, e2s, e2r, e3s, e3r, cs4, cr4, e4s, e4r, epr,
+    e0s, e0r, cr1, e1s, e1r, e2s, e2r, e3s, e3r, cs4, cr4, e4s, e4r, epr, posv,
     partq, sibr, sendq, recvq, acc1, acc2, pd2, pd1, pdm, halfs, r1, r2, gd, xsend, xrecv,
     asend, arecv, dsend, drecv, outq, outd,
     x_s, x_r, e0_s, e0_r, e1_s, e1_r, e2_s, e2_r, e3_s, e3_r, e4_s, e4_r, ep_s, ep_r,
@@ -112,6 +112,12 @@
 
     sub8 = lambda n: lax.broadcasted_iota(jnp.int32, (8, n), 0)
 
+    posv[...] = jnp.zeros_like(posv)
+    for seg in range(3):
+        at = slice(128 * seg, min(128 * (seg + 1), ROWS))
+        width = at.stop - at.start
+        posv[seg : seg + 1, 0:width] = (pos[:, at] // 128).astype(f32)
+        posv[3 + seg : 4 + seg, 0:width] = (pos[:, at] % 128).astype(f32)
     for c in sources:
         c.wait()
     nq = xq[...].astype(f32) * gain[...]
@@ -302,37 +308,45 @@
     for k in range(NCH):
         normalise(0, k, y)
     astart(0)
-    ep = (pos, epr, ep_s, ep_r, 8, hz, by_hz)
+    ep = (posv, epr, ep_s, ep_r, 8, hz, by_hz)
     exchange(*ep)
     for k in range(NCH):
         yrecv(0, k, 0)
         begun(ycopy(0, k, 2))
         yrecv(0, k, 1)
         begun(ycopy(0, k, 3))
+    for k in range(NCH):
         pack(1, k)
         begun(ycopy(1, k, 0))
         begun(ycopy(1, k, 1))
+    for k in range(NCH):
         normalise(0, k, (y + 3) % 4)
         normalise(0, k, (y + 1) % 4)
     astart(1)
     astart(2)
     amid(0)
     for k in range(NCH):
-        normalise(1, k, y)
         yrecv(0, k, 2)
         yrecv(0, k, 3)
         normalise(0, k, (y + 2) % 4)
     astart(3)
+    for k in range(NCH):
+        normalise(1, k, y)
     alast(0)
     amid(1)
     amid(2)
-    for k in range(NCH):
+
+    def docs_on(k):
         yrecv(1, k, 0)
         begun(ycopy(1, k, 2))
         yrecv(1, k, 1)
         begun(ycopy(1, k, 3))
+
+    docs_on(0)
     alast(1)
+    docs_on(1)
     alast(2)
+    docs_on(2)
     for k in range(NCH):
         normalise(1, k, (y + 3) % 4)
         normalise(1, k, (y + 1) % 4)
@@ -604,23 +618,23 @@
         return jnp.sum(g * eq, axis=1, keepdims=True)
 
     part_q(0)
+    part_q(1)
+    q_far(0)
+    part_q(2)
+    q_far(1)
     gc[0].wait_recv()
     pd1[front] = (acc1[...] + halfs[0].astype(f32)).astype(bf16)
     begun(gc[4])
     gc[1].wait_recv()
     pdm[rear] = (acc2[...] + halfs[1].astype(f32)).astype(bf16)
     begun(gc[5])
-    part_q(1)
-    q_far(0)
-    part_q(2)
-    q_far(1)
+    q_far(2)
     part_q(3)
     q_near(0)
-    q_far(2)
     q_near(1)
+    q_near(2)
     q_direct(3)
     q_across(0)
-    q_near(2)
     for i in range(2, 6):
         gc[i].wait_recv()
     gd[...] = gd[...] + r1[...].astype(f32) + r2[...].astype(f32)
@@ -710,6 +724,13 @@
         wait()
 
 
+def results(gq, gdoc, ggain, loss, oq, od, ogain, oloss):
+    oq[...] = gq[...]
+    od[...] = gdoc[...]
+    ogain[...] = ggain[...]
+    oloss[...] = loss[...]
+
+
 def shards(query_states, doc_states, gain, positives):
     vm = pl.BlockSpec(memory_space=pltpu.VMEM)
     hbm = pl.BlockSpec(memory_space=pl.ANY)
@@ -727,7 +748,7 @@
         S((8, ROWS), f32), S((TP, 8, ROWS), f32),
         S((8, ROWS), f32), S((TP, 8, ROWS), f32),
         S((8, FEATS), f32), S((8, FEATS), f32), S((8, FEATS), f32), S((8, 8, FEATS), f32),
-        S((DP, 8, 128), f32),
+        S((DP, 8, 128), f32), S((8, 128), f32),
         S((TAKE + TILE, FULL), bf16), S((8, 3 * TILE, FULL), bf16),
         S((7, 3 * TILE, FULL), bf16), S((7, 3 * TILE, FULL), bf16),
         S((ROWS // 2, WIDE), f32), S((ROWS // 2, WIDE), f32),
@@ -742,8 +763,6 @@
         + pair(8 * NCH) + pair(64) + [dma(4)] + pair(32) + pair(32) + pair(7) + pair(TP) + pair(TP)
         + pair(3) + [dma(2)]
     )
-    padded = jnp.pad(positives, (0, 3 * 128 - ROWS)).reshape(3, 128)
-    parts = jnp.concatenate([padded // 128, padded % 128, jnp.zeros((2, 128), jnp.int32)])
     gq, gdoc, ggain, loss = pl.pallas_call(
         step,
         name="infonce_step",
@@ -762,7 +781,19 @@
         cost_estimate=pl.CostEstimate(
             flops=7_000_000_000, bytes_accessed=3_000_000, transcendentals=1_000_000
         ),
-    )(query_states, doc_states, gain[None, :], parts.astype(f32))
+    )(query_states, doc_states, gain[None, :], positives[None, :])
+    gq, gdoc, ggain, loss = pl.pallas_call(
+        results,
+        name="results",
+        out_shape=(
+            jax.ShapeDtypeStruct((ROWS, FEATS), bf16),
+            jax.ShapeDtypeStruct((ROWS, FEATS), bf16),
+            jax.ShapeDtypeStruct((1, FEATS), f32),
+            jax.ShapeDtypeStruct((1, 1), f32),
+        ),
+        in_specs=[vm] * 4,
+        out_specs=(vm,) * 4,
+    )(gq, gdoc, ggain, loss)
     return gq, gdoc, ggain[0], loss[0, 0]
 
 

time: 127 us -> 123 us (0.969)
  local copies, waits for them, and re-layouts: 3.71 us -> 1.25 us
  between operations: 2.43 us -> 0.64 us
    unnamed x9 -> x0, local copies, waits for them, and re-layouts: 3.63 us -> none
    pallas_call x0 -> x1, Pallas kernels: none -> 2.45 us  [shards(): pl.pallas_call(results, name='results', out_shape=(jax.ShapeDtypeStruct((...]
    pallas_call x1, Pallas kernels: 120 us -> 117 us  [shards(): pl.pallas_call(step, name='infonce_step', out_shape=(jax.ShapeDtypeStruct...]
where the time goes in v5:
time: 123 us; the launch traced here: 122 us
  Pallas kernels  120 us (98%)
  local copies, waits for them, and re-layouts  1.25 us (1%)
    pallas_call x1, Pallas kernels, shards(): pl.pallas_call(step, name='infonce_step', out_shape=(jax.ShapeDtypeStruct...  117 us

profile of v5, /device:TPU:1, one launch (start us, length us, event | category | flops | bytes accessed | tf_op | source)
XLA Modules:
  0.0 121.5 jit_solution(4560009658385864079)
XLA Ops:
  0.6 1.2 %broadcast_in_dim.7.pos = s32[1,288]{1,0:T(1,128)} reshape(s32[288]{0:T(512)} %param.7) | data formatting | bytes 2304 | tf_op jit(solution)/shard_map/broadcast_in_dim | solution.py:784
  1.9 117.2 %infonce_step.1 = (bf16[288,448]{1,0:T(8,128)(2,1)}, bf16[288,448]{1,0:T(8,128)(2,1)}, f32[1,448]{1,0:T(1,128)}, f32[1,1]{1,0:T(1,128)}) custom-call(bf16[288,448]{1,0:T(8,128)(2,1)} %hq.1, bf16[288,448]{1,0:T(8,128)(2,1)} %hd.1, f32[1,448]{1,0:T(1,128)} %bitcast.3, s32[1,288]{1,0:T(1,128)} %broadcast_in_dim.7.pos), custom_call_target="tpu_custom_call" | custom-call | flops 7000000000 | bytes 3000000 | tf_op jit(solution)/shard_map/infonce_step/pallas_call | solution.py:766
  119.1 2.5 %results.1 = (bf16[288,448]{1,0:T(8,128)(2,1)}, bf16[288,448]{1,0:T(8,128)(2,1)}, f32[1,448]{1,0:T(1,128)}, f32[1,1]{1,0:T(1,128)}) custom-call(bf16[288,448]{1,0:T(8,128)(2,1)} %get-tuple-element.12.gq, bf16[288,448]{1,0:T(8,128)(2,1)} %get-tuple-element.13.gdoc, f32[1,448]{1,0:T(1,128)} %get-tuple-element.14.ggain, f32[1,1]{1,0:T(1,128)} %get-tuple-element.15.loss), custom_call_target="tpu_custom_call" | custom-call | tf_op jit(solution)/shard_map/results/pallas_call | solution.py:785

commit v6 on v5

--- a/solution.py
+++ b/solution.py
@@ -36,9 +36,9 @@
     xq, xd, pq, pd, gfull, raw, emb, qi, invq, invd, logits, stat, wts, wtt,
     e0s, e0r, cr1, e1s, e1r, e2s, e2r, e3s, e3r, cs4, cr4, e4s, e4r, epr, posv,
     partq, sibr, sendq, recvq, acc1, acc2, pd2, pd1, pdm, halfs, r1, r2, gd, xsend, xrecv,
-    asend, arecv, dsend, drecv, outq, outd,
+    asend, arecv, pick, cs5, cr5, e5s, e5r, outq, outd,
     x_s, x_r, e0_s, e0_r, e1_s, e1_r, e2_s, e2_r, e3_s, e3_r, e4_s, e4_r, ep_s, ep_r,
-    y_s, y_r, a_s, a_r, loc, b_s, b_r, u_s, u_r, g_s, g_r, t_s, t_r, v_s, v_r, c_s, c_r, io,
+    y_s, y_r, a_s, a_r, loc, b_s, b_r, u_s, u_r, g_s, g_r, t_s, t_r, e5_s, e5_r, c_s, c_r, io,
 ):
     d = lax.axis_index("dp")
     t = lax.axis_index("tensor")
@@ -118,6 +118,47 @@
         width = at.stop - at.start
         posv[seg : seg + 1, 0:width] = (pos[:, at] // 128).astype(f32)
         posv[3 + seg : 4 + seg, 0:width] = (pos[:, at] % 128).astype(f32)
+    pl.semaphore_wait(barrier, TP + 7)
+
+    def xcopy(i):
+        src, dst = (hq, pq) if i < NCH else (hd, pd)
+        part = pl.ds((i % NCH) * CHUNK, CHUNK)
+        return copy(src.at[part], dst.at[part], x_s.at[i], x_r.at[i], partner)
+
+    def begun(c):
+        c.start()
+        sent.append(c.wait_send)
+
+    def exchange(src, recv, ss, rs, size, me, dev):
+        @pl.loop(1, size)
+        def _(k):
+            copy(src, recv.at[me], ss.at[k], rs.at[me], dev((me + k) % size)).start()
+
+        @sent.append
+        def _():
+            @pl.loop(1, size)
+            def _(k):
+                copy(src, recv.at[me], ss.at[k], rs.at[me], dev((me + k) % size)).wait_send()
+
+    def finish(src, recv, ss, rs, size, me, dev):
+        recv[me] = src[...]
+
+        @pl.loop(1, size)
+        def _(k):
+            s = (me + k) % size
+            copy(src, recv.at[s], ss.at[k], rs.at[s], dev(s)).wait_recv()
+
+    by_tensor = lambda s: (d, s)
+    by_hz = lambda s: (s * 2 + core, t)
+
+    def total(recv, size):
+        acc = recv[0]
+        for s in range(1, size):
+            acc = acc + recv[s]
+        return acc
+
+    e0 = (e0s, e0r, e0_s, e0_r, TP, t, by_tensor)
+    begun(xcopy(0))
     for c in sources:
         c.wait()
     nq = xq[...].astype(f32) * gain[...]
@@ -127,47 +168,6 @@
     e0s[...] = jnp.broadcast_to(gain[...], (8, FEATS))
     e0s[0:1, 0:ROWS] = lq[0:1]
     e0s[1:2, 0:ROWS] = ld[0:1]
-    pl.semaphore_wait(barrier, TP + 7)
-
-    def xcopy(i):
-        src, dst = (xq, pq) if i < NCH else (xd, pd)
-        part = pl.ds((i % NCH) * CHUNK, CHUNK)
-        return copy(src.at[part], dst.at[part], x_s.at[i], x_r.at[i], partner)
-
-    def begun(c):
-        c.start()
-        sent.append(c.wait_send)
-
-    def exchange(src, recv, ss, rs, size, me, dev):
-        @pl.loop(1, size)
-        def _(k):
-            copy(src, recv.at[me], ss.at[k], rs.at[me], dev((me + k) % size)).start()
-
-        @sent.append
-        def _():
-            @pl.loop(1, size)
-            def _(k):
-                copy(src, recv.at[me], ss.at[k], rs.at[me], dev((me + k) % size)).wait_send()
-
-    def finish(src, recv, ss, rs, size, me, dev):
-        recv[me] = src[...]
-
-        @pl.loop(1, size)
-        def _(k):
-            s = (me + k) % size
-            copy(src, recv.at[s], ss.at[k], rs.at[s], dev(s)).wait_recv()
-
-    by_tensor = lambda s: (d, s)
-    by_hz = lambda s: (s * 2 + core, t)
-
-    def total(recv, size):
-        acc = recv[0]
-        for s in range(1, size):
-            acc = acc + recv[s]
-        return acc
-
-    e0 = (e0s, e0r, e0_s, e0_r, TP, t, by_tensor)
-    begun(xcopy(0))
     exchange(*e0)
     for i in range(1, 2 * NCH):
         begun(xcopy(i))
@@ -423,7 +423,7 @@
     e1s[...] = jnp.where(sub_t == 0, top_c, jnp.where(sub_t == 1, tot, posit + cr1[2:3]))
     e1 = (e1s, e1r, e1_s, e1_r, 8, hz, by_hz)
     exchange(*e1)
-    pick = jnp.where(own_j == row_p, 1.0, 0.0).astype(bf16)
+    pick[...] = jnp.where(own_j == row_p, 1.0, 0.0).astype(bf16)
     finish(*e1)
     all_top = e1r[0, 0:1]
     for s in range(1, 8):
@@ -436,17 +436,21 @@
     lse = all_top + jnp.log(all_tot)
     loss_part = jnp.sum(lse - all_pos, axis=1, keepdims=True)
 
-    lse1 = lse.astype(bf16).astype(f32)
-    lse2 = (lse - lse1).astype(bf16).astype(f32)
-    split = jnp.where(
-        sub_t == 0, lse1, jnp.where(sub_t == 1, lse2, jnp.where(sub_t == 2, lse - lse1 - lse2, 0.0))
-    )
-    lse_own = jnp.sum(
-        lax.dot_general(
-            split.astype(bf16), pick, (((1,), (1,)), ((), ())), preferred_element_type=f32
-        ),
-        axis=0, keepdims=True,
-    )
+    def own_lanes(vec):
+        p1 = vec.astype(bf16).astype(f32)
+        p2 = (vec - p1).astype(bf16).astype(f32)
+        split = jnp.where(
+            sub_t == 0, p1, jnp.where(sub_t == 1, p2, jnp.where(sub_t == 2, vec - p1 - p2, 0.0))
+        )
+        return jnp.sum(
+            lax.dot_general(
+                split.astype(bf16), pick[...], (((1,), (1,)), ((), ())),
+                preferred_element_type=f32,
+            ),
+            axis=0, keepdims=True,
+        )
+
+    lse_own = own_lanes(lse)
     e2s[...] = jnp.where(sub8(ROWS) == 0, lse_own, loss_part)
     e2 = (e2s, e2r, e2_s, e2_r, TP, t, by_tensor)
     exchange(*e2)
@@ -492,6 +496,12 @@
     wts[ROWS:] = (wq + wt).astype(bf16)
     wtt[...] = jnp.transpose(wts[...])
 
+    weighed = wts[...].astype(f32) * logits[...]
+    cs5[...] = jnp.broadcast_to(jnp.sum(weighed, axis=0, keepdims=True), (8, TAKE))
+    c5 = copy(cs5, cr5, c_s.at[3], c_r.at[3], sibling)
+    begun(c5)
+    e3s[...] = to_lanes(jnp.sum(weighed[0:ROWS], axis=1, keepdims=True))
+
     def target(s):
         return (xh + s // 4) % 2 * 4 + (zc + s % 4) % 4
 
@@ -614,12 +624,14 @@
                 sent.append(
                     lambda far=far: sized(extra, lambda n: tcopy(f, far, n).wait_send())
                 )
-        eq = emb[pl.ds(pl.multiple_of(ROWS + mine * TILE, TILE), N3), lanes(fb)].astype(f32)
-        return jnp.sum(g * eq, axis=1, keepdims=True)
 
     part_q(0)
     part_q(1)
     q_far(0)
+    c5.wait_recv()
+    e5s[...] = cs5[...] + cr5[...]
+    e5 = (e5s, e5r, e5_s, e5_r, 8, hz, by_hz)
+    exchange(*e5)
     part_q(2)
     q_far(1)
     gc[0].wait_recv()
@@ -634,6 +646,10 @@
     q_near(1)
     q_near(2)
     q_direct(3)
+    finish(*e5)
+    e3s[0:1] = own_lanes(total(e5r, 8)[0:1])
+    e3 = (e3s, e3r, e3_s, e3_r, TP, t, by_tensor)
+    exchange(*e3)
     q_across(0)
     for i in range(2, 6):
         gc[i].wait_recv()
@@ -641,53 +657,26 @@
     xsend[...] = jnp.where(low == 0, gd[:, FEATS:], gd[:, :FEATS]).astype(bf16)
     begun(gc[6])
     q_across(1)
-    dots = q_own(0)
+    q_own(0)
     q_across(2)
-    dots = dots + q_own(1)
+    q_own(1)
 
     gc[6].wait_recv()
     gd[:, 0:FEATS] = jnp.where(low == 0, gd[:, :FEATS], gd[:, FEATS:]) + xrecv[...].astype(f32)
-    fd = jnp.sum(gd[:, 0:FEATS] * (xd[...].astype(f32) * gain[...]), axis=1, keepdims=True)
-    e3s[...] = to_lanes(fd)
-    e3 = (e3s, e3r, e3_s, e3_r, TP, t, by_tensor)
-    exchange(*e3)
-    dots = dots + q_own(2)
-
-    dots = dots + q_own(3)
-    dsend[...] = jnp.broadcast_to(dots, (N3, 128))
-
-    def vcopy(k, n):
-        to = (t + k) % TP
-        return copy(
-            dsend.at[pl.ds(0, n)], drecv.at[rows_at(mine, n)], v_s.at[k], v_r.at[k], (d, to)
-        )
-
-    def vrecv(k, n):
-        s = (t + TP - k) % TP
-        at = drecv.at[rows_at(begin(d4, s), n)]
-        return copy(at, at, v_s.at[k], v_r.at[k], (d, s))
-
-    @pl.loop(1, TP)
-    def _(k):
-        sized(extra, lambda n: vcopy(k, n).start())
-
-    @sent.append
-    def _():
-        @pl.loop(1, TP)
-        def _(k):
-            sized(extra, lambda n: vcopy(k, n).wait_send())
+    q_own(2)
+    q_own(3)
 
     def tlocal(n):
         arecv[rows_at(mine, n)] = asend[t, pl.ds(0, n)]
-        drecv[rows_at(mine, n)] = dsend[pl.ds(0, n)]
 
     sized(extra, tlocal)
 
     finish(*e3)
-    col = to_rows(total(e3r, TP)[0:1])[:, 0:1]
+    dots = total(e3r, TP)
+    col = to_rows(dots[1:2])[:, 0:1]
     iv = invd[:, 0:1]
     h = xd[...].astype(f32)
-    gx = iv * gd[:, 0:FEATS] - h * gain[...] * (iv * iv * iv * col)
+    gx = iv * gd[:, 0:FEATS] - h * gain[...] * (iv * iv * col)
     outd[...] = (gx * gain[...]).astype(bf16)
     outs = [pltpu.make_async_copy(outd, od, io.at[0]), pltpu.make_async_copy(outq, oq, io.at[1])]
     outs[0].start()
@@ -698,13 +687,10 @@
             if f < 3 or far == 1:
                 trecv(f, far)
 
-    @pl.loop(1, TP)
-    def _(k):
-        sized(d4 == ((t + TP - k) % TP) // 2, lambda n: vrecv(k, n).wait_recv())
-
+    col = to_rows(dots[0:1])[:, 0:1]
     h = xq[...].astype(f32)
     iv = invq[0:ROWS, 0:1]
-    gx = iv * arecv[...].astype(f32) - h * gain[...] * (iv * iv * drecv[:, 0:1])
+    gx = iv * arecv[...].astype(f32) - h * gain[...] * (iv * iv * col)
     gg = gg + jnp.sum(gx * h, axis=0, keepdims=True)
     cs4[...] = jnp.broadcast_to(gg, (8, FEATS))
     c4 = copy(cs4, cr4, c_s.at[2], c_r.at[2], sibling)
@@ -724,11 +710,13 @@
         wait()
 
 
-def results(gq, gdoc, ggain, loss, oq, od, ogain, oloss):
-    oq[...] = gq[...]
-    od[...] = gdoc[...]
-    ogain[...] = ggain[...]
-    oloss[...] = loss[...]
+def results(gq, gdoc, ggain, loss, oq, od, ogain, oloss, sems):
+    pairs = ((gq, oq), (gdoc, od), (ggain, ogain), (loss, oloss))
+    copies = [pltpu.make_async_copy(a, b, sems.at[i]) for i, (a, b) in enumerate(pairs)]
+    for c in copies:
+        c.start()
+    for c in copies:
+        c.wait()
 
 
 def shards(query_states, doc_states, gain, positives):
@@ -755,13 +743,14 @@
         S((ROWS, WIDE), bf16), S((ROWS, WIDE), bf16), S((ROWS, WIDE), bf16),
         S((2, ROWS // 2, WIDE), bf16), S((ROWS, WIDE), bf16), S((ROWS, WIDE), bf16),
         S((ROWS, WIDE), f32), S((ROWS, FEATS), bf16), S((ROWS, FEATS), bf16),
-        S((TP, 3 * TILE, FEATS), bf16), S((ROWS, FEATS), bf16), S((3 * TILE, 128), f32), S((ROWS, 128), f32),
+        S((TP, 3 * TILE, FEATS), bf16), S((ROWS, FEATS), bf16), S((ROWS, TAKE), bf16),
+        S((8, TAKE), f32), S((8, TAKE), f32), S((8, TAKE), f32), S((8, 8, TAKE), f32),
         S((ROWS, FEATS), bf16), S((ROWS, FEATS), bf16),
     ]
     sems = (
         pair(2 * NCH) + pair(TP) + pair(8) + pair(TP) + pair(TP) + pair(8) + pair(8)
-        + pair(8 * NCH) + pair(64) + [dma(4)] + pair(32) + pair(32) + pair(7) + pair(TP) + pair(TP)
-        + pair(3) + [dma(2)]
+        + pair(8 * NCH) + pair(64) + [dma(4)] + pair(32) + pair(32) + pair(7) + pair(TP) + pair(8)
+        + pair(4) + [dma(2)]
     )
     gq, gdoc, ggain, loss = pl.pallas_call(
         step,
@@ -791,8 +780,9 @@
             jax.ShapeDtypeStruct((1, FEATS), f32),
             jax.ShapeDtypeStruct((1, 1), f32),
         ),
-        in_specs=[vm] * 4,
-        out_specs=(vm,) * 4,
+        in_specs=[hbm] * 4,
+        out_specs=(hbm,) * 4,
+        scratch_shapes=[dma(4)],
     )(gq, gdoc, ggain, loss)
     return gq, gdoc, ggain[0], loss[0, 0]
 

time: 123 us -> 140 us (1.14); the launches traced: 122 us -> 140 us
  Pallas kernels: 120 us -> 138 us
    pallas_call x1, Pallas kernels: 2.45 us -> 19.6 us  [shards(): pl.pallas_call(results, name='results', out_shape=(jax.ShapeDtypeStruct((...]
where the time goes in v6:
time: 140 us
  Pallas kernels  138 us (99%)
    pallas_call x1, Pallas kernels, shards(): pl.pallas_call(step, name='infonce_step', out_shape=(jax.ShapeDtypeStruct...  118 us
    pallas_call x1, Pallas kernels, shards(): pl.pallas_call(results, name='results', out_shape=(jax.ShapeDtypeStruct((...  19.6 us

profile of v6, /device:TPU:1, one launch (start us, length us, event | category | flops | bytes accessed | tf_op | source)
XLA Modules:
  0.0 140.1 jit_solution(16126298344303354346)
XLA Ops:
  0.6 1.2 broadcast_in_dim.7.pos
  1.9 118.4 %infonce_step.1 = (bf16[288,448]{1,0:T(8,128)(2,1)}, bf16[288,448]{1,0:T(8,128)(2,1)}, f32[1,448]{1,0:T(1,128)}, f32[1,1]{1,0:T(1,128)}) custom-call(bf16[288,448]{1,0:T(8,128)(2,1)} %hq.1, bf16[288,448]{1,0:T(8,128)(2,1)} %hd.1, f32[1,448]{1,0:T(1,128)} %bitcast.3, s32[1,288]{1,0:T(1,128)} %broadcast_in_dim.7.pos), custom_call_target="tpu_custom_call" | custom-call | flops 7000000000 | bytes 3000000 | tf_op jit(solution)/shard_map/infonce_step/pallas_call | solution.py:755
  120.3 19.6 %results.1 = (bf16[288,448]{1,0:T(8,128)(2,1)}, bf16[288,448]{1,0:T(8,128)(2,1)}, f32[1,448]{1,0:T(1,128)}, f32[1,1]{1,0:T(1,128)}) custom-call(bf16[288,448]{1,0:T(8,128)(2,1)} %get-tuple-element.12.gq, bf16[288,448]{1,0:T(8,128)(2,1)} %get-tuple-element.13.gdoc, f32[1,448]{1,0:T(1,128)} %get-tuple-element.14.ggain, f32[1,1]{1,0:T(1,128)} %get-tuple-element.15.loss), custom_call_target="tpu_custom_call" | custom-call | tf_op jit(solution)/shard_map/results/pallas_call | solution.py:774

commit v7 on v6

--- a/solution.py
+++ b/solution.py
@@ -34,7 +34,7 @@
     hq, hd, gain, pos,
     oq, od, ogain, oloss,
     xq, xd, pq, pd, gfull, raw, emb, qi, invq, invd, logits, stat, wts, wtt,
-    e0s, e0r, cr1, e1s, e1r, e2s, e2r, e3s, e3r, cs4, cr4, e4s, e4r, epr, posv,
+    e0s, e0r, cs1, cr1, e1s, e1r, e2s, e2r, e3s, e3r, cs4, cr4, e4s, e4r, epr, posv,
     partq, sibr, sendq, recvq, acc1, acc2, pd2, pd1, pdm, halfs, r1, r2, gd, xsend, xrecv,
     asend, arecv, pick, cs5, cr5, e5s, e5r, outq, outd,
     x_s, x_r, e0_s, e0_r, e1_s, e1_r, e2_s, e2_r, e3_s, e3_r, e4_s, e4_r, ep_s, ep_r,
@@ -104,6 +104,20 @@
         )
 
     pl.semaphore_signal(barrier, inc=1, device_id=sibling, device_id_type=MESH)
+    def fold(ref, row, vec):
+        for k in range(-(-vec.shape[1] // 128)):
+            part = vec[:, 128 * k : 128 * (k + 1)]
+            ref[row + k : row + k + 1, 0 : part.shape[1]] = part
+
+    def unfold(tile, row, size):
+        return jnp.concatenate(
+            [
+                tile[row + k : row + k + 1, 0 : min(128, size - 128 * k)]
+                for k in range(-(-size // 128))
+            ],
+            axis=1,
+        )
+
     def to_lanes(col):
         return jnp.transpose(jnp.broadcast_to(col, (ROWS, 128)))[:8]
 
@@ -413,28 +427,33 @@
     statistics(logits[0:ROWS])
 
     sub_t = sub8(TAKE)
-    c1 = copy(stat, cr1, c_s.at[1], c_r.at[1], sibling)
+    cs1[...] = jnp.zeros_like(cs1)
+    for i in range(3):
+        fold(cs1, 5 * i, stat[i : i + 1])
+    c1 = copy(cs1, cr1, c_s.at[1], c_r.at[1], sibling)
     begun(c1)
     c1.wait_recv()
-    top, tot, posit = stat[0:1], stat[1:2], stat[2:3]
-    top_o = cr1[0:1]
+    top, top_o = cs1[0:5], cr1[0:5]
     top_c = jnp.maximum(top, top_o)
-    tot = tot * jnp.exp(top - top_c) + cr1[1:2] * jnp.exp(top_o - top_c)
-    e1s[...] = jnp.where(sub_t == 0, top_c, jnp.where(sub_t == 1, tot, posit + cr1[2:3]))
+    e1s[0:5] = top_c
+    e1s[5:10] = cs1[5:10] * jnp.exp(top - top_c) + cr1[5:10] * jnp.exp(top_o - top_c)
+    e1s[10:15] = cs1[10:15] + cr1[10:15]
+    e1s[15:16] = jnp.zeros((1, 128), f32)
     e1 = (e1s, e1r, e1_s, e1_r, 8, hz, by_hz)
     exchange(*e1)
     pick[...] = jnp.where(own_j == row_p, 1.0, 0.0).astype(bf16)
     finish(*e1)
-    all_top = e1r[0, 0:1]
+    all_top = e1r[0, 0:5]
     for s in range(1, 8):
-        all_top = jnp.maximum(all_top, e1r[s, 0:1])
+        all_top = jnp.maximum(all_top, e1r[s, 0:5])
     all_tot = jnp.zeros_like(all_top)
     all_pos = jnp.zeros_like(all_top)
     for s in range(8):
-        all_tot = all_tot + e1r[s, 1:2] * jnp.exp(e1r[s, 0:1] - all_top)
-        all_pos = all_pos + e1r[s, 2:3]
-    lse = all_top + jnp.log(all_tot)
-    loss_part = jnp.sum(lse - all_pos, axis=1, keepdims=True)
+        all_tot = all_tot + e1r[s, 5:10] * jnp.exp(e1r[s, 0:5] - all_top)
+        all_pos = all_pos + e1r[s, 10:15]
+    lse = unfold(all_top, 0, TAKE) + jnp.log(unfold(all_tot, 0, TAKE))
+    loss_part = jnp.sum(lse - unfold(all_pos, 0, TAKE), axis=1, keepdims=True)
+    sub_t = sub8(TAKE)
 
     def own_lanes(vec):
         p1 = vec.astype(bf16).astype(f32)
@@ -451,7 +470,8 @@
         )
 
     lse_own = own_lanes(lse)
-    e2s[...] = jnp.where(sub8(ROWS) == 0, lse_own, loss_part)
+    e2s[...] = jnp.broadcast_to(loss_part, (8, 128))
+    fold(e2s, 0, lse_own)
     e2 = (e2s, e2r, e2_s, e2_r, TP, t, by_tensor)
     exchange(*e2)
     wd = (jnp.exp(logits[0:ROWS] - lse) - (own_j == pos_p).astype(f32)) * (1.0 / PAIRS)
@@ -489,18 +509,20 @@
 
     finish(*e2)
     sums = total(e2r, TP)
-    oloss[...] = sums[1:2, 0:1] * (1.0 / PAIRS)
-    lse_j = to_rows(sums[0:1])[:, 0:1]
+    oloss[...] = sums[3:4, 0:1] * (1.0 / PAIRS)
+    lse_j = to_rows(unfold(sums, 0, ROWS))[:, 0:1]
     wq = (jnp.exp(logits[ROWS:] - lse) * (1.0 / PAIRS)).astype(bf16).astype(f32)
     wt = (jnp.exp(logits[ROWS:] - lse_j) * (1.0 / PAIRS)).astype(bf16).astype(f32)
     wts[ROWS:] = (wq + wt).astype(bf16)
     wtt[...] = jnp.transpose(wts[...])
 
     weighed = wts[...].astype(f32) * logits[...]
-    cs5[...] = jnp.broadcast_to(jnp.sum(weighed, axis=0, keepdims=True), (8, TAKE))
+    cs5[...] = jnp.zeros_like(cs5)
+    fold(cs5, 0, jnp.sum(weighed, axis=0, keepdims=True))
     c5 = copy(cs5, cr5, c_s.at[3], c_r.at[3], sibling)
     begun(c5)
-    e3s[...] = to_lanes(jnp.sum(weighed[0:ROWS], axis=1, keepdims=True))
+    e3s[...] = jnp.zeros_like(e3s)
+    fold(e3s, 3, to_lanes(jnp.sum(weighed[0:ROWS], axis=1, keepdims=True))[0:1])
 
     def target(s):
         return (xh + s // 4) % 2 * 4 + (zc + s % 4) % 4
@@ -647,7 +669,7 @@
     q_near(2)
     q_direct(3)
     finish(*e5)
-    e3s[0:1] = own_lanes(total(e5r, 8)[0:1])
+    fold(e3s, 0, own_lanes(unfold(total(e5r, 8), 0, TAKE)))
     e3 = (e3s, e3r, e3_s, e3_r, TP, t, by_tensor)
     exchange(*e3)
     q_across(0)
@@ -673,7 +695,7 @@
 
     finish(*e3)
     dots = total(e3r, TP)
-    col = to_rows(dots[1:2])[:, 0:1]
+    col = to_rows(unfold(dots, 3, ROWS))[:, 0:1]
     iv = invd[:, 0:1]
     h = xd[...].astype(f32)
     gx = iv * gd[:, 0:FEATS] - h * gain[...] * (iv * iv * col)
@@ -687,12 +709,13 @@
             if f < 3 or far == 1:
                 trecv(f, far)
 
-    col = to_rows(dots[0:1])[:, 0:1]
+    col = to_rows(unfold(dots, 0, ROWS))[:, 0:1]
     h = xq[...].astype(f32)
     iv = invq[0:ROWS, 0:1]
     gx = iv * arecv[...].astype(f32) - h * gain[...] * (iv * iv * col)
     gg = gg + jnp.sum(gx * h, axis=0, keepdims=True)
-    cs4[...] = jnp.broadcast_to(gg, (8, FEATS))
+    cs4[...] = jnp.zeros_like(cs4)
+    fold(cs4, 0, gg)
     c4 = copy(cs4, cr4, c_s.at[2], c_r.at[2], sibling)
     begun(c4)
     outq[...] = (gx * gain[...]).astype(bf16)
@@ -702,7 +725,7 @@
     e4 = (e4s, e4r, e4_s, e4_r, 8, hz, by_hz)
     exchange(*e4)
     finish(*e4)
-    ogain[...] = total(e4r, 8)[0:1]
+    ogain[...] = unfold(total(e4r, 8), 0, FEATS)
     for c in outs:
         c.wait()
 
@@ -710,13 +733,11 @@
         wait()
 
 
-def results(gq, gdoc, ggain, loss, oq, od, ogain, oloss, sems):
-    pairs = ((gq, oq), (gdoc, od), (ggain, ogain), (loss, oloss))
-    copies = [pltpu.make_async_copy(a, b, sems.at[i]) for i, (a, b) in enumerate(pairs)]
-    for c in copies:
-        c.start()
-    for c in copies:
-        c.wait()
+def results(gq, gdoc, ggain, loss, oq, od, ogain, oloss):
+    oq[...] = gq[...]
+    od[...] = gdoc[...]
+    ogain[...] = ggain[...]
+    oloss[...] = loss[...]
 
 
 def shards(query_states, doc_states, gain, positives):
@@ -732,10 +753,10 @@
         S((ROWS + TILE, 128), f32), S((ROWS, 128), f32),
         S((2 * ROWS, TAKE), f32), S((8, TAKE), f32), S((2 * ROWS, TAKE), bf16), S((TAKE, 2 * ROWS), bf16),
         S((8, FEATS), f32), S((TP, 8, FEATS), f32),
-        S((8, TAKE), f32), S((8, TAKE), f32), S((8, 8, TAKE), f32),
-        S((8, ROWS), f32), S((TP, 8, ROWS), f32),
-        S((8, ROWS), f32), S((TP, 8, ROWS), f32),
-        S((8, FEATS), f32), S((8, FEATS), f32), S((8, FEATS), f32), S((8, 8, FEATS), f32),
+        S((16, 128), f32), S((16, 128), f32), S((16, 128), f32), S((8, 16, 128), f32),
+        S((8, 128), f32), S((TP, 8, 128), f32),
+        S((8, 128), f32), S((TP, 8, 128), f32),
+        S((8, 128), f32), S((8, 128), f32), S((8, 128), f32), S((8, 8, 128), f32),
         S((DP, 8, 128), f32), S((8, 128), f32),
         S((TAKE + TILE, FULL), bf16), S((8, 3 * TILE, FULL), bf16),
         S((7, 3 * TILE, FULL), bf16), S((7, 3 * TILE, FULL), bf16),
@@ -744,7 +765,7 @@
         S((2, ROWS // 2, WIDE), bf16), S((ROWS, WIDE), bf16), S((ROWS, WIDE), bf16),
         S((ROWS, WIDE), f32), S((ROWS, FEATS), bf16), S((ROWS, FEATS), bf16),
         S((TP, 3 * TILE, FEATS), bf16), S((ROWS, FEATS), bf16), S((ROWS, TAKE), bf16),
-        S((8, TAKE), f32), S((8, TAKE), f32), S((8, TAKE), f32), S((8, 8, TAKE), f32),
+        S((8, 128), f32), S((8, 128), f32), S((8, 128), f32), S((8, 8, 128), f32),
         S((ROWS, FEATS), bf16), S((ROWS, FEATS), bf16),
     ]
     sems = (
@@ -780,9 +801,8 @@
             jax.ShapeDtypeStruct((1, FEATS), f32),
             jax.ShapeDtypeStruct((1, 1), f32),
         ),
-        in_specs=[hbm] * 4,
-        out_specs=(hbm,) * 4,
-        scratch_shapes=[dma(4)],
+        in_specs=[vm] * 4,
+        out_specs=(vm,) * 4,
     )(gq, gdoc, ggain, loss)
     return gq, gdoc, ggain[0], loss[0, 0]
 

time: 140 us -> 120 us (0.86)
  Pallas kernels: 138 us -> 118 us
    pallas_call x1, Pallas kernels: 19.6 us -> 2.45 us  [shards(): pl.pallas_call(results, name='results', out_shape=(jax.ShapeDtypeStruct((...]
    pallas_call x1, Pallas kernels: 118 us -> 115 us  [shards(): pl.pallas_call(step, name='infonce_step', out_shape=(jax.ShapeDtypeStruct...]
where the time goes in v7:
time: 120 us
  Pallas kernels  118 us (98%)
  local copies, waits for them, and re-layouts  1.25 us (1%)
    pallas_call x1, Pallas kernels, shards(): pl.pallas_call(step, name='infonce_step', out_shape=(jax.ShapeDtypeStruct...  115 us
    pallas_call x1, Pallas kernels, shards(): pl.pallas_call(results, name='results', out_shape=(jax.ShapeDtypeStruct((...  2.45 us

profile of v7, /device:TPU:1, one launch (start us, length us, event | category | flops | bytes accessed | tf_op | source)
XLA Modules:
  0.0 119.7 jit_solution(1258575148029931798)
XLA Ops:
  0.6 1.2 %broadcast_in_dim.7.pos = s32[1,288]{1,0:T(1,128)} reshape(s32[288]{0:T(512)} %param.7) | data formatting | bytes 2304 | tf_op jit(solution)/shard_map/broadcast_in_dim | solution.py:794
  1.9 115.3 %infonce_step.1 = (bf16[288,448]{1,0:T(8,128)(2,1)}, bf16[288,448]{1,0:T(8,128)(2,1)}, f32[1,448]{1,0:T(1,128)}, f32[1,1]{1,0:T(1,128)}) custom-call(bf16[288,448]{1,0:T(8,128)(2,1)} %hq.1, bf16[288,448]{1,0:T(8,128)(2,1)} %hd.1, f32[1,448]{1,0:T(1,128)} %bitcast.3, s32[1,288]{1,0:T(1,128)} %broadcast_in_dim.7.pos), custom_call_target="tpu_custom_call" | custom-call | flops 7000000000 | bytes 3000000 | tf_op jit(solution)/shard_map/infonce_step/pallas_call | solution.py:776
  117.2 2.5 %results.1 = (bf16[288,448]{1,0:T(8,128)(2,1)}, bf16[288,448]{1,0:T(8,128)(2,1)}, f32[1,448]{1,0:T(1,128)}, f32[1,1]{1,0:T(1,128)}) custom-call(bf16[288,448]{1,0:T(8,128)(2,1)} %get-tuple-element.12.gq, bf16[288,448]{1,0:T(8,128)(2,1)} %get-tuple-element.13.gdoc, f32[1,448]{1,0:T(1,128)} %get-tuple-element.14.ggain, f32[1,1]{1,0:T(1,128)} %get-tuple-element.15.loss), custom_call_target="tpu_custom_call" | custom-call | tf_op jit(solution)/shard_map/results/pallas_call | solution.py:795

commit v8 on v7

--- a/solution.py
+++ b/solution.py
@@ -130,8 +130,8 @@
     for seg in range(3):
         at = slice(128 * seg, min(128 * (seg + 1), ROWS))
         width = at.stop - at.start
-        posv[seg : seg + 1, 0:width] = (pos[:, at] // 128).astype(f32)
-        posv[3 + seg : 4 + seg, 0:width] = (pos[:, at] % 128).astype(f32)
+        posv[seg : seg + 1, 0:width] = (pos[at] // 128).astype(f32)[None, :]
+        posv[3 + seg : 4 + seg, 0:width] = (pos[at] % 128).astype(f32)[None, :]
     pl.semaphore_wait(barrier, TP + 7)
 
     def xcopy(i):
@@ -505,7 +505,6 @@
     pdm[front] = gd[front].astype(bf16)
     begun(gc[3])
     acc2[...] = gd[rear]
-    gd[...] = part_d(y)
 
     finish(*e2)
     sums = total(e2r, TP)
@@ -515,14 +514,6 @@
     wt = (jnp.exp(logits[ROWS:] - lse_j) * (1.0 / PAIRS)).astype(bf16).astype(f32)
     wts[ROWS:] = (wq + wt).astype(bf16)
     wtt[...] = jnp.transpose(wts[...])
-
-    weighed = wts[...].astype(f32) * logits[...]
-    cs5[...] = jnp.zeros_like(cs5)
-    fold(cs5, 0, jnp.sum(weighed, axis=0, keepdims=True))
-    c5 = copy(cs5, cr5, c_s.at[3], c_r.at[3], sibling)
-    begun(c5)
-    e3s[...] = jnp.zeros_like(e3s)
-    fold(e3s, 3, to_lanes(jnp.sum(weighed[0:ROWS], axis=1, keepdims=True))[0:1])
 
     def target(s):
         return (xh + s // 4) % 2 * 4 + (zc + s % 4) % 4
@@ -650,12 +641,20 @@
     part_q(0)
     part_q(1)
     q_far(0)
+
+    weighed = wts[...].astype(f32) * logits[...]
+    cs5[...] = jnp.zeros_like(cs5)
+    fold(cs5, 0, jnp.sum(weighed, axis=0, keepdims=True))
+    c5 = copy(cs5, cr5, c_s.at[3], c_r.at[3], sibling)
+    begun(c5)
+    e3s[...] = jnp.zeros_like(e3s)
+    fold(e3s, 3, to_lanes(jnp.sum(weighed[0:ROWS], axis=1, keepdims=True))[0:1])
+    part_q(2)
+    q_far(1)
     c5.wait_recv()
     e5s[...] = cs5[...] + cr5[...]
     e5 = (e5s, e5r, e5_s, e5_r, 8, hz, by_hz)
     exchange(*e5)
-    part_q(2)
-    q_far(1)
     gc[0].wait_recv()
     pd1[front] = (acc1[...] + halfs[0].astype(f32)).astype(bf16)
     begun(gc[4])
@@ -668,6 +667,7 @@
     q_near(1)
     q_near(2)
     q_direct(3)
+    gd[...] = part_d(y)
     finish(*e5)
     fold(e3s, 0, own_lanes(unfold(total(e5r, 8), 0, TAKE)))
     e3 = (e3s, e3r, e3_s, e3_r, TP, t, by_tensor)
@@ -791,7 +791,7 @@
         cost_estimate=pl.CostEstimate(
             flops=7_000_000_000, bytes_accessed=3_000_000, transcendentals=1_000_000
         ),
-    )(query_states, doc_states, gain[None, :], positives[None, :])
+    )(query_states, doc_states, gain[None, :], positives)
     gq, gdoc, ggain, loss = pl.pallas_call(
         results,
         name="results",

time: 120 us -> 118 us (0.983)
  local copies, waits for them, and re-layouts: 1.25 us -> 0 us
    broadcast_in_dim x1 -> x0, local copies, waits for them, and re-layouts: 1.25 us -> none  [shards(): positives[None, :]]
where the time goes in v8:
time: 118 us
  Pallas kernels  117 us (99%)
    pallas_call x1, Pallas kernels, shards(): pl.pallas_call(step, name='infonce_step', out_shape=(jax.ShapeDtypeStruct...  115 us
    pallas_call x1, Pallas kernels, shards(): pl.pallas_call(results, name='results', out_shape=(jax.ShapeDtypeStruct((...  2.45 us

profile of v8, /device:TPU:1, one launch (start us, length us, event | category | flops | bytes accessed | tf_op | source)
XLA Modules:
  0.0 118.1 jit_solution(3358931843468344137)
XLA Ops:
  0.6 115.0 %infonce_step.1 = (bf16[288,448]{1,0:T(8,128)(2,1)}, bf16[288,448]{1,0:T(8,128)(2,1)}, f32[1,448]{1,0:T(1,128)}, f32[1,1]{1,0:T(1,128)}) custom-call(bf16[288,448]{1,0:T(8,128)(2,1)} %hq.1, bf16[288,448]{1,0:T(8,128)(2,1)} %hd.1, f32[1,448]{1,0:T(1,128)} %bitcast.3, s32[288]{0:T(512)} %pos.1), custom_call_target="tpu_custom_call" | custom-call | flops 7000000000 | bytes 3000000 | tf_op jit(solution)/shard_map/infonce_step/pallas_call | solution.py:776
  115.7 2.5 %results.1 = (bf16[288,448]{1,0:T(8,128)(2,1)}, bf16[288,448]{1,0:T(8,128)(2,1)}, f32[1,448]{1,0:T(1,128)}, f32[1,1]{1,0:T(1,128)}) custom-call(bf16[288,448]{1,0:T(8,128)(2,1)} %get-tuple-element.12.gq, bf16[288,448]{1,0:T(8,128)(2,1)} %get-tuple-element.13.gdoc, f32[1,448]{1,0:T(1,128)} %get-tuple-element.14.ggain, f32[1,1]{1,0:T(1,128)} %get-tuple-element.15.loss), custom_call_target="tpu_custom_call" | custom-call | tf_op jit(solution)/shard_map/results/pallas_call | solution.py:795

commit v9 on v8

--- a/solution.py
+++ b/solution.py
@@ -63,6 +63,10 @@
 
     sent = []
 
+    def drain(count):
+        for _ in range(min(count, len(sent))):
+            sent.pop(0)()
+
     def copy(src, dst, ss, rs, dev):
         return pltpu.make_async_remote_copy(
             src_ref=src, dst_ref=dst, send_sem=ss, recv_sem=rs, device_id=dev, device_id_type=MESH
@@ -432,6 +436,7 @@
         fold(cs1, 5 * i, stat[i : i + 1])
     c1 = copy(cs1, cr1, c_s.at[1], c_r.at[1], sibling)
     begun(c1)
+    drain(30)
     c1.wait_recv()
     top, top_o = cs1[0:5], cr1[0:5]
     top_c = jnp.maximum(top, top_o)
@@ -441,6 +446,7 @@
     e1s[15:16] = jnp.zeros((1, 128), f32)
     e1 = (e1s, e1r, e1_s, e1_r, 8, hz, by_hz)
     exchange(*e1)
+    drain(60)
     pick[...] = jnp.where(own_j == row_p, 1.0, 0.0).astype(bf16)
     finish(*e1)
     all_top = e1r[0, 0:5]
@@ -720,17 +726,18 @@
     begun(c4)
     outq[...] = (gx * gain[...]).astype(bf16)
     outs[1].start()
+    drain(30)
     c4.wait_recv()
     e4s[...] = cs4[...] + cr4[...]
     e4 = (e4s, e4r, e4_s, e4_r, 8, hz, by_hz)
     exchange(*e4)
+    drain(len(sent))
     finish(*e4)
     ogain[...] = unfold(total(e4r, 8), 0, FEATS)
     for c in outs:
         c.wait()
 
-    for wait in sent:
-        wait()
+    drain(len(sent))
 
 
 def results(gq, gdoc, ggain, loss, oq, od, ogain, oloss):

time: 118 us -> 117 us (level)
  no operation moved by 1% of the time
where the time goes in v9:
time: 117 us
  Pallas kernels  117 us (100%)
    pallas_call x1, Pallas kernels, shards(): pl.pallas_call(step, name='infonce_step', out_shape=(jax.ShapeDtypeStruct...  114 us
    pallas_call x1, Pallas kernels, shards(): pl.pallas_call(results, name='results', out_shape=(jax.ShapeDtypeStruct((...  2.45 us

profile of v9, /device:TPU:1, one launch (start us, length us, event | category | flops | bytes accessed | tf_op | source)
XLA Modules:
  0.0 117.2 jit_solution(7027304301669992663)
XLA Ops:
  0.6 114.1 %infonce_step.1 = (bf16[288,448]{1,0:T(8,128)(2,1)}, bf16[288,448]{1,0:T(8,128)(2,1)}, f32[1,448]{1,0:T(1,128)}, f32[1,1]{1,0:T(1,128)}) custom-call(bf16[288,448]{1,0:T(8,128)(2,1)} %hq.1, bf16[288,448]{1,0:T(8,128)(2,1)} %hd.1, f32[1,448]{1,0:T(1,128)} %bitcast.3, s32[288]{0:T(512)} %pos.1), custom_call_target="tpu_custom_call" | custom-call | flops 7000000000 | bytes 3000000 | tf_op jit(solution)/shard_map/infonce_step/pallas_call | solution.py:783
  114.8 2.5 %results.1 = (bf16[288,448]{1,0:T(8,128)(2,1)}, bf16[288,448]{1,0:T(8,128)(2,1)}, f32[1,448]{1,0:T(1,128)}, f32[1,1]{1,0:T(1,128)}) custom-call(bf16[288,448]{1,0:T(8,128)(2,1)} %get-tuple-element.12.gq, bf16[288,448]{1,0:T(8,128)(2,1)} %get-tuple-element.13.gdoc, f32[1,448]{1,0:T(1,128)} %get-tuple-element.14.ggain, f32[1,1]{1,0:T(1,128)} %get-tuple-element.15.loss), custom_call_target="tpu_custom_call" | custom-call | tf_op jit(solution)/shard_map/results/pallas_call | solution.py:802

commit v10 on v9

--- a/solution.py
+++ b/solution.py
@@ -25,7 +25,7 @@
 PAIRS = DP * ROWS
 TAKE = DP * ROWS // TP
 TILE = 16
-CHUNK = 96
+CHUNK = 32
 NCH = ROWS // CHUNK
 HALF = CHUNK // 2
 
@@ -360,11 +360,15 @@
         yrecv(1, k, 1)
         begun(ycopy(1, k, 3))
 
-    docs_on(0)
+    third_k = NCH // 3
+    for k in range(third_k):
+        docs_on(k)
     alast(1)
-    docs_on(1)
+    for k in range(third_k, 2 * third_k):
+        docs_on(k)
     alast(2)
-    docs_on(2)
+    for k in range(2 * third_k, NCH):
+        docs_on(k)
     for k in range(NCH):
         normalise(1, k, (y + 3) % 4)
         normalise(1, k, (y + 1) % 4)
@@ -436,7 +440,7 @@
         fold(cs1, 5 * i, stat[i : i + 1])
     c1 = copy(cs1, cr1, c_s.at[1], c_r.at[1], sibling)
     begun(c1)
-    drain(30)
+    drain(50)
     c1.wait_recv()
     top, top_o = cs1[0:5], cr1[0:5]
     top_c = jnp.maximum(top, top_o)
@@ -446,7 +450,7 @@
     e1s[15:16] = jnp.zeros((1, 128), f32)
     e1 = (e1s, e1r, e1_s, e1_r, 8, hz, by_hz)
     exchange(*e1)
-    drain(60)
+    drain(110)
     pick[...] = jnp.where(own_j == row_p, 1.0, 0.0).astype(bf16)
     finish(*e1)
     all_top = e1r[0, 0:5]

time: 117 us -> 119 us (1.017)
    pallas_call x1, Pallas kernels: 114 us -> 116 us  [shards(): pl.pallas_call(step, name='infonce_step', out_shape=(jax.ShapeDtypeStruct...]
where the time goes in v10:
time: 119 us
  Pallas kernels  118 us (99%)
    pallas_call x1, Pallas kernels, shards(): pl.pallas_call(step, name='infonce_step', out_shape=(jax.ShapeDtypeStruct...  116 us
    pallas_call x1, Pallas kernels, shards(): pl.pallas_call(results, name='results', out_shape=(jax.ShapeDtypeStruct((...  2.45 us

profile of v10, /device:TPU:1, one launch (start us, length us, event | category | flops | bytes accessed | tf_op | source)
XLA Modules:
  0.0 118.7 jit_solution(17981538297239233596)
XLA Ops:
  0.6 115.6 %infonce_step.1 = (bf16[288,448]{1,0:T(8,128)(2,1)}, bf16[288,448]{1,0:T(8,128)(2,1)}, f32[1,448]{1,0:T(1,128)}, f32[1,1]{1,0:T(1,128)}) custom-call(bf16[288,448]{1,0:T(8,128)(2,1)} %hq.1, bf16[288,448]{1,0:T(8,128)(2,1)} %hd.1, f32[1,448]{1,0:T(1,128)} %bitcast.3, s32[288]{0:T(512)} %pos.1), custom_call_target="tpu_custom_call" | custom-call | flops 7000000000 | bytes 3000000 | tf_op jit(solution)/shard_map/infonce_step/pallas_call | solution.py:787
  116.3 2.5 %results.1 = (bf16[288,448]{1,0:T(8,128)(2,1)}, bf16[288,448]{1,0:T(8,128)(2,1)}, f32[1,448]{1,0:T(1,128)}, f32[1,1]{1,0:T(1,128)}) custom-call(bf16[288,448]{1,0:T(8,128)(2,1)} %get-tuple-element.12.gq, bf16[288,448]{1,0:T(8,128)(2,1)} %get-tuple-element.13.gdoc, f32[1,448]{1,0:T(1,128)} %get-tuple-element.14.ggain, f32[1,1]{1,0:T(1,128)} %get-tuple-element.15.loss), custom_call_target="tpu_custom_call" | custom-call | tf_op jit(solution)/shard_map/results/pallas_call | solution.py:806
